TPU v7x, 128 devices: a whole 4x4x4 slice. The times are simulated.
128 devices in a mesh: lat: 8 (over z, x_lo), lon: 16 (over y, x_hi, core).
Axes of the slice: x: 4 (x_hi: 2, x_lo: 2; x = x_hi * 2 + x_lo), y: 4, z: 4, core: 2. Of those that a mesh axis runs over, the one named last changes fastest.
Arguments:
- activations: bfloat16 [192, 768, 512], P('lat', 'lon'), may hold values from -6 to 6
- cotangent: bfloat16 [192, 768, 512], P('lat', 'lon'), may hold values from -6 to 6
- norm_gain: float32 [512], replicated, may hold values from 0.1 to 1.9
- qkv_weight: bfloat16 [512, 1536], replicated, may hold values from -12 to 12
- proj_weight: bfloat16 [512, 512], replicated, may hold values from -0.25 to 0.25
Outputs:
- grad_input: bfloat16 [192, 768, 512], P('lat', 'lon')
- grad_qkv: float32 [512, 1536], P(('lat', 'lon'))
- grad_proj: float32 [512, 512], P(('lat', 'lon'))
- grad_gain: float32 [512], P(('lat', 'lon'))
All inputs are finite; a program needn't handle non-finite values.
Results may differ from a plain program's by a relative error of at most 0.0059.
The roundings to bfloat16 on the way count: a program that leaves them out, or rounds other values in their place, can miss the bound.
Values may be sent and summed in bfloat16 or wider, within the bound.
A program may use at most 128 MiB of HBM per device.

v0:
```python
import math

import jax
import jax.numpy as jnp
from jax import lax
from jax.sharding import PartitionSpec as P

HEADS = 16
WIN_LAT = 6
WIN_LON = 12


def shifted(shard, axis, by):
    peers = lax.axis_size(axis)
    return lax.ppermute(shard, axis, [(i, (i + by) % peers) for i in range(peers)])


def window_grads(win_in, win_cot, win_region, norm_gain, qkv_weight, proj_weight):
    n_windows, win_span, channels = win_in.shape
    head_size = channels // HEADS
    scale = head_size ** (-0.5)
    tokens_f = win_in.astype(jnp.float32).reshape(n_windows * win_span, channels)
    center = tokens_f - jnp.mean(tokens_f, axis=-1, keepdims=True)
    inv_std = lax.rsqrt(jnp.mean(center * center, axis=-1, keepdims=True) + 1e-05)
    normed = center * inv_std
    scaled_in = (normed * norm_gain).astype(jnp.bfloat16)
    qkv_all = jnp.dot(scaled_in, qkv_weight, preferred_element_type=jnp.float32).astype(
        jnp.bfloat16
    )
    qkv_all = qkv_all.reshape(n_windows, win_span, 3, HEADS, head_size)
    query = qkv_all[:, :, 0]
    key_heads = qkv_all[:, :, 1]
    val_heads = qkv_all[:, :, 2]
    scores = (
        jnp.einsum("bqhd,bkhd->bhqk", query, key_heads, preferred_element_type=jnp.float32) * scale
    )
    allowed = (win_region[:, :, None] == win_region[:, None, :])[:, None]
    scores = jnp.where(allowed, scores, -1e30)
    row_max = jnp.max(scores, axis=-1, keepdims=True)
    expon = jnp.exp(scores - row_max)
    prob = expon / jnp.sum(expon, axis=-1, keepdims=True)
    prob_b = prob.astype(jnp.bfloat16)
    attended = jnp.einsum("bhqk,bkhd->bqhd", prob_b, val_heads, preferred_element_type=jnp.float32)
    attended = attended.astype(jnp.bfloat16).reshape(n_windows * win_span, channels)
    cot_flat = win_cot.reshape(n_windows * win_span, channels)
    grad_proj = jnp.einsum("tc,te->ce", attended, cot_flat, preferred_element_type=jnp.float32)
    grad_att = jnp.einsum("tc,ec->te", cot_flat, proj_weight, preferred_element_type=jnp.float32)
    grad_att = grad_att.astype(jnp.bfloat16).reshape(n_windows, win_span, HEADS, head_size)
    grad_prob = jnp.einsum(
        "bqhd,bkhd->bhqk", grad_att, val_heads, preferred_element_type=jnp.float32
    )
    grad_val = jnp.einsum(
        "bhqk,bqhd->bkhd", prob_b, grad_att, preferred_element_type=jnp.float32
    ).astype(jnp.bfloat16)
    inner = jnp.sum(prob * grad_prob, axis=-1, keepdims=True)
    grad_score = (prob * (grad_prob - inner) * scale).astype(jnp.bfloat16)
    grad_query = jnp.einsum(
        "bhqk,bkhd->bqhd", grad_score, key_heads, preferred_element_type=jnp.float32
    ).astype(jnp.bfloat16)
    grad_key = jnp.einsum(
        "bhqk,bqhd->bkhd", grad_score, query, preferred_element_type=jnp.float32
    ).astype(jnp.bfloat16)
    grad_all = jnp.stack([grad_query, grad_key, grad_val], axis=2).reshape(
        n_windows * win_span, 3 * channels
    )
    grad_qkv = jnp.einsum("tc,te->ce", scaled_in, grad_all, preferred_element_type=jnp.float32)
    grad_normed = jnp.einsum("te,ce->tc", grad_all, qkv_weight, preferred_element_type=jnp.float32)
    grad_gain = jnp.sum(grad_normed * normed, axis=0)
    grad_hat = grad_normed * norm_gain
    branch = inv_std * (
        grad_hat
        - jnp.mean(grad_hat, axis=-1, keepdims=True)
        - normed * jnp.mean(grad_hat * normed, axis=-1, keepdims=True)
    )
    return (branch.reshape(n_windows, win_span, channels), grad_qkv, grad_proj, grad_gain)


def to_windows(field, slab_rows, slab_cols):
    channels = field.shape[-1]
    blocks = field.reshape(slab_rows // WIN_LAT, WIN_LAT, slab_cols // WIN_LON, WIN_LON, channels)
    return blocks.transpose(0, 2, 1, 3, 4).reshape(-1, WIN_LAT * WIN_LON, channels)


def from_windows(blocks, slab_rows, slab_cols):
    channels = blocks.shape[-1]
    grid = blocks.reshape(slab_rows // WIN_LAT, slab_cols // WIN_LON, WIN_LAT, WIN_LON, channels)
    return grid.transpose(0, 2, 1, 3, 4).reshape(slab_rows, slab_cols, channels)


def on_device(activations, cotangent, norm_gain, qkv_weight, proj_weight):
    slab_rows, slab_cols, channels = activations.shape
    half_lat = WIN_LAT // 2
    half_lon = WIN_LON // 2
    upper_rows = shifted((activations[:half_lat], cotangent[:half_lat]), "lat", -1)
    ext_in = jnp.concatenate([activations, upper_rows[0]], axis=0)
    ext_cot = jnp.concatenate([cotangent, upper_rows[1]], axis=0)
    side_cols = shifted((ext_in[:, :half_lon], ext_cot[:, :half_lon]), "lon", -1)
    ext_in = jnp.concatenate([ext_in, side_cols[0]], axis=1)
    ext_cot = jnp.concatenate([ext_cot, side_cols[1]], axis=1)
    moved_in = ext_in[half_lat:, half_lon:]
    moved_cot = ext_cot[half_lat:, half_lon:]
    total_rows = slab_rows * lax.axis_size("lat")
    global_row = lax.axis_index("lat") * slab_rows + jnp.arange(slab_rows, dtype=jnp.int32)
    row_region = (global_row >= total_rows - half_lat).astype(jnp.int32)
    region_grid = jnp.broadcast_to(row_region[:, None, None], (slab_rows, slab_cols, 1))
    win_region = to_windows(region_grid, slab_rows, slab_cols)[:, :, 0]
    branch, grad_qkv, grad_proj, grad_gain = window_grads(
        to_windows(moved_in, slab_rows, slab_cols),
        to_windows(moved_cot, slab_rows, slab_cols),
        win_region,
        norm_gain,
        qkv_weight,
        proj_weight,
    )
    grad_back = from_windows(branch, slab_rows, slab_cols)
    right_cols = shifted(grad_back[:, slab_cols - half_lon :], "lon", 1)
    grad_back = jnp.concatenate([right_cols, grad_back[:, : slab_cols - half_lon]], axis=1)
    lower_rows = shifted(grad_back[slab_rows - half_lat :], "lat", 1)
    grad_back = jnp.concatenate([lower_rows, grad_back[: slab_rows - half_lat]], axis=0)
    grad_input = (cotangent.astype(jnp.float32) + grad_back).astype(jnp.bfloat16)
    token_scale = 1.0 / math.sqrt(
        slab_rows * slab_cols * lax.axis_size("lat") * lax.axis_size("lon")
    )
    reduced = (
        lax.psum_scatter(grad_qkv, ("lat", "lon"), scatter_dimension=0, tiled=True),
        lax.psum_scatter(grad_proj, ("lat", "lon"), scatter_dimension=0, tiled=True),
        lax.psum_scatter(grad_gain, ("lat", "lon"), scatter_dimension=0, tiled=True),
    )
    return (
        grad_input,
        reduced[0] * token_scale,
        reduced[1] * token_scale,
        reduced[2] * token_scale,
    )


def solution(mesh):
    return jax.shard_map(
        on_device,
        mesh=mesh,
        in_specs=(P("lat", "lon", None), P("lat", "lon", None), P(), P(), P()),
        out_specs=(
            P("lat", "lon", None),
            P(("lat", "lon"), None),
            P(("lat", "lon"), None),
            P(("lat", "lon")),
        ),
        check_vma=False,
    )
```

profile of v0, /device:TPU:0, one launch (start us, length us, event | category | flops | bytes accessed | tf_op | source)
XLA Modules:
  0.0 369.1 jit_solution(2902318115795957956)
XLA Ops:
  8.3 5.1 %collective-permute-start = (bf16[3,48,512]{2,1,0:T(8,128)(2,1)S(1)}, bf16[3,48,512]{2,1,0:T(8,128)(2,1)S(1)}, u32[]{:S(2)}, u32[]{:S(2)}) collective-permute-start(bf16[3,48,512]{2,1,0:T(8,128)(2,1)S(1)} %slice.39), channel_id=1, source_target_pairs={{0,112},{16,0},{32,16},{48,32},{64,48},{80,64},{96,80},{112,96},{1... | collective-permute-start | bytes 442376 | tf_op jit(solution)/shard_map/ppermute | solution.py:15
  17.7 4.1 %collective-permute-start.1 = (bf16[27,6,512]{2,1,0:T(8,128)(2,1)S(1)}, bf16[27,6,512]{2,1,0:T(8,128)(2,1)S(1)}, u32[]{:S(2)}, u32[]{:S(2)}) collective-permute-start(bf16[27,6,512]{2,1,0:T(8,128)(2,1)S(1)} %slice.52), channel_id=1, source_target_pairs={{0,15},{1,0},{2,1},{3,2},{4,3},{5,4},{6,5},{7,6},{8,7},{9,8},{10,9... | collective-permute-start | bytes 497672 | tf_op jit(solution)/shard_map/ppermute | solution.py:15
  34.6 4.1 %copy.40 = f32[4,4,6,12,512]{4,3,2,1,0:T(8,128)} copy(f32[4,4,6,12,512]{4,3,1,2,0:T(8,128)} %bitcast.54) | data formatting | bytes 4718592 | tf_op jit(solution)/shard_map/convert_element_type | solution.py:22
  42.6 5.5 %convolution_convert_fusion = bf16[1152,1536]{1,0:T(8,128)(2,1)} fusion(bf16[512,1536]{1,0:T(8,128)(2,1)S(1)} %copy-done, f32[1152,512]{1,0:T(8,128)} %reshape.116, f32[512]{0:T(512)S(1)} %copy-done.13, f32[1152]{0:T(1024)S(1)} %div.24, f32[1152]{0:T(1024)S(1)} %rsqrt.13), kind=kOutput, calls=%fused_computation.7 | convolution fusion | flops 1816068096 | bytes 7482368 | tf_op jit(solution)/shard_map/dot_general | solution.py:27
  48.1 5.8 %copy.42 = bf16[1152,1536]{0,1:T(8,128)(2,1)} copy(bf16[1152,1536]{1,0:T(8,128)(2,1)} %convolution_convert_fusion) | data formatting | bytes 7077888 | tf_op jit(solution)/shard_map/convert_element_type | solution.py:27
  53.9 13.6 %reshape.110 = bf16[16,72,3,16,32]{1,0,4,3,2:T(8,128)(2,1)} reshape(bf16[1152,1536]{0,1:T(8,128)(2,1)} %copy.42) | data formatting | bytes 7077888 | tf_op jit(solution)/shard_map/reshape | solution.py:30
  67.5 6.5 %fusion.45 = (bf16[16,72,1,16,32]{1,0,4,3,2:T(8,128)(2,1)}, bf16[16,72,1,16,32]{1,0,4,3,2:T(8,128)(2,1)}, bf16[16,72,1,16,32]{1,0,4,3,2:T(8,128)(2,1)}) fusion(bf16[16,72,3,16,32]{1,0,4,3,2:T(8,128)(2,1)} %reshape.110), kind=kLoop, calls=%fused_computation.72 | loop fusion | bytes 7077888 | tf_op jit(solution)/shard_map/slice | solution.py:33
  87.9 4.7 %reshape.112 = bf16[16,72,16,32]{1,0,3,2:T(8,128)(2,1)} reshape(bf16[1152,512]{0,1:T(8,128)(2,1)S(1)} %copy.46) | data formatting | bytes 2359296 | tf_op jit(solution)/shard_map/reshape | solution.py:48
  92.5 4.9 %fusion.30 = f32[16,16,72,72]{2,3,1,0:T(8,128)S(1)} fusion(bf16[16,72,1,16,32]{1,0,4,3,2:T(8,128)(2,1)} %get-tuple-element.11, bf16[16,72,1,16,32]{1,0,4,3,2:T(8,128)(2,1)} %get-tuple-element.10), kind=kOutput, calls=%fused_computation.40 | convolution fusion | flops 84934656 | bytes 7667712 | tf_op jit(solution)/shard_map/bqhd,bkhd->bhqk/dot_general | solution.py:35
  97.5 5.3 %fusion.46 = (f32[16,16,72]{2,1,0:T(8,128)S(1)}, f32[16,16,72,72]{2,3,1,0:T(8,128)}) fusion(f32[16,16,72,72]{2,3,1,0:T(8,128)S(1)} %fusion.30, pred[16,72,72]{1,2,0:T(8,128)(4,1)S(1)} %copy-done.12), kind=kOutput, calls=%fused_computation.73 | output fusion | flops 7962695 | bytes 10773504 | tf_op jit(solution)/shard_map/sub | solution.py:40
  102.8 5.9 %fusion.31 = f32[16,16,72,72]{2,3,1,0:T(8,128)} fusion(bf16[16,72,1,16,32]{1,0,4,3,2:T(8,128)(2,1)S(1)} %copy-done.5, bf16[16,72,16,32]{1,0,3,2:T(8,128)(2,1)S(1)} %copy-done.4), kind=kOutput, calls=%fused_computation.41 | convolution fusion | flops 84934656 | bytes 7667712 | tf_op jit(solution)/shard_map/bqhd,bkhd->bhqk/dot_general | solution.py:49
  112.5 17.0 %convert_bitcast_fusion.3 = bf16[16,72,1,16,32]{1,4,3,0,2:T(8,128)(2,1)} fusion(f32[16,16,72,72]{2,3,1,0:T(8,128)} %fusion.31, bf16[16,72,1,16,32]{1,0,4,3,2:T(8,128)(2,1)} %get-tuple-element.11, f32[16,16,72,72]{2,3,1,0:T(8,128)} %get-tuple-element.13, f32[16,16,72]{2,1,0:T(8,128)S(1)} %get-tuple-element.12), kind=kOutput, calls=%fused_computation.38 | convolution fusion | flops 94832712 | bytes 13049856 | tf_op jit(solution)/shard_map/bhqk,bkhd->bqhd/dot_general | solution.py:57
  129.6 16.5 %convert_bitcast_fusion.2 = bf16[16,72,1,16,32]{1,4,3,0,2:T(8,128)(2,1)} fusion(f32[16,16,72,72]{2,3,1,0:T(8,128)} %fusion.31, bf16[16,72,1,16,32]{1,0,4,3,2:T(8,128)(2,1)} %get-tuple-element.10, f32[16,16,72,72]{2,3,1,0:T(8,128)} %get-tuple-element.13, f32[16,16,72]{2,1,0:T(8,128)S(1)} %get-tuple-element.12), kind=kOutput, calls=%fused_computation.37 | convolution fusion | flops 94832712 | bytes 13049856 | tf_op jit(solution)/shard_map/bhqk,bqhd->bkhd/dot_general | solution.py:60
  146.1 8.4 %convert_bitcast_fusion.1 = bf16[16,72,1,16,32]{1,4,3,0,2:T(8,128)(2,1)} fusion(bf16[16,72,16,32]{1,0,3,2:T(8,128)(2,1)} %reshape.112, f32[16,16,72,72]{2,3,1,0:T(8,128)} %get-tuple-element.13, f32[16,16,72]{2,1,0:T(8,128)S(1)} %get-tuple-element.12), kind=kOutput, calls=%fused_computation.36 | convolution fusion | flops 88178688 | bytes 7741440 | tf_op jit(solution)/shard_map/bhqk,bqhd->bkhd/dot_general | solution.py:52
  158.8 5.0 %reshape.115 = bf16[1152,512]{0,1:T(8,128)(2,1)} reshape(bf16[16,72,16,32]{1,0,3,2:T(8,128)(2,1)} %copy.57) | data formatting | bytes 2359296 | tf_op jit(solution)/shard_map/reshape | solution.py:44
  170.5 9.9 %copy.53 = bf16[16,72,3,16,32]{1,0,4,3,2:T(8,128)(2,1)} copy(bf16[16,72,3,16,32]{1,4,3,0,2:T(8,128)(2,1)S(1)} %pad_maximum_fusion) | data formatting | bytes 7077888 | tf_op jit(solution)/shard_map/stack | solution.py:63
  180.4 10.7 %reshape.113 = bf16[1152,1536]{0,1:T(8,128)(2,1)} reshape(bf16[16,72,3,16,32]{1,0,4,3,2:T(8,128)(2,1)} %copy.53) | data formatting | bytes 7077888 | tf_op jit(solution)/shard_map/reshape | solution.py:63
  194.9 6.0 %fusion.47 = f32[512,1536]{1,0:T(8,128)} fusion(bf16[1152,512]{1,0:T(8,128)(2,1)S(1)} %convert_element_type.97, bf16[1152,1536]{0,1:T(8,128)(2,1)} %reshape.113), kind=kOutput, calls=%fused_computation.74 | convolution fusion | flops 1811939328 | bytes 7864320 | tf_op jit(solution)/shard_map/tc,te->ce/dot_general | solution.py:66
  200.9 5.9 %multiply_reduce_fusion.2 = (f32[512]{0:T(512)S(1)}, f32[1152]{0:T(1024)S(1)}, f32[1152]{0:T(1024)S(1)}, f32[1152,512]{1,0:T(8,128)S(1)}) fusion(f32[1152,512]{1,0:T(8,128)} %reshape.116, f32[1152]{0:T(1024)S(1)} %div.24, f32[1152]{0:T(1024)S(1)} %rsqrt.13, f32[512]{0:T(512)S(1)} %copy-done.13, bf16[1152,1536]{0,1:T(8,128)(2,1)} %reshape.113, ...), kind=kOutput, calls=%fused_computation.23 | convolution fusion | flops 1816655104 | bytes 9852928 | tf_op jit(solution)/shard_map/te,ce->tc/dot_general | solution.py:67
  212.8 4.1 %copy.54 = f32[4,6,4,12,512]{4,3,2,1,0:T(8,128)} copy(f32[4,6,4,12,512]{4,3,1,2,0:T(8,128)} %bitcast.57) | data formatting | bytes 4718592 | tf_op jit(solution)/shard_map/transpose | solution.py:87
  216.9 4.0 %reshape.114 = f32[24,48,512]{2,1,0:T(8,128)} reshape(f32[4,6,4,12,512]{4,3,2,1,0:T(8,128)} %copy.54) | data formatting | bytes 4718592 | tf_op jit(solution)/shard_map/reshape | solution.py:87
  222.1 12.9 %collective-permute-done.4 = f32[24,6,512]{2,1,0:T(8,128)S(1)} collective-permute-done((f32[24,6,512]{2,1,0:T(8,128)S(1)}, f32[24,6,512]{2,1,0:T(8,128)S(1)}, u32[]{:S(2)}, u32[]{:S(2)}) %collective-permute-start.4) | collective-permute-done | bytes 294944 | tf_op jit(solution)/shard_map/ppermute | solution.py:15
  236.3 64.5 %all-reduce.2 = f32[512]{0:T(512)S(1)} all-reduce(f32[512]{0:T(512)S(1)} %get-tuple-element.4), channel_id=4, replica_groups=mesh['lat'=8,'lon'=16] {'lat','lon'}, use_global_device_ids=true, to_apply=%region_10.11.clone | all-reduce | flops 512 | bytes 4096
  304.4 54.9 %all-reduce.6.cloned.1.call-done = (f32[512,1536]{1,0:T(8,128)}, f32[512,512]{1,0:T(8,128)}) async-done(((f32[512,1536]{1,0:T(8,128)}, f32[512,512]{1,0:T(8,128)}), (f32[512,1536]{1,0:T(8,128)}, f32[512,512]{1,0:T(8,128)})) %all-reduce.6.cloned.1.call-update) | async-done | bytes 4194320
  (86 shorter events, 69.3 us)
Async XLA Ops:
  7.2 35.5 %copy-start = (bf16[512,1536]{1,0:T(8,128)(2,1)S(1)}, bf16[512,1536]{1,0:T(8,128)(2,1)}, u32[]{:S(2)}) copy-start(bf16[512,1536]{1,0:T(8,128)(2,1)} %param.8) | copy-start | bytes 4718596
  7.2 352.2 %all-reduce.6.cloned.1.call-start = ((), (), s32[]{:S(2)}) async-start(), calls=%async_computation | async-start | bytes 8388608
  8.3 9.4 %collective-permute-start = (bf16[3,48,512]{2,1,0:T(8,128)(2,1)S(1)}, bf16[3,48,512]{2,1,0:T(8,128)(2,1)S(1)}, u32[]{:S(2)}, u32[]{:S(2)}) collective-permute-start(bf16[3,48,512]{2,1,0:T(8,128)(2,1)S(1)} %slice.39), channel_id=1, source_target_pairs={{0,112},{16,0},{32,16},{48,32},{64,48},{80,64},{96,80},{112,96},{1... | collective-permute-start | bytes 442376 | tf_op jit(solution)/shard_map/ppermute | solution.py:15
  14.3 7.6 %collective-permute-start.2 = (bf16[3,48,512]{2,1,0:T(8,128)(2,1)S(1)}, bf16[3,48,512]{2,1,0:T(8,128)(2,1)S(1)}, u32[]{:S(2)}, u32[]{:S(2)}) collective-permute-start(bf16[3,48,512]{2,1,0:T(8,128)(2,1)S(1)} %slice.44), channel_id=1, source_target_pairs={{0,112},{16,0},{32,16},{48,32},{64,48},{80,64},{96,80},{112,96},{1... | collective-permute-start | bytes 442376 | tf_op jit(solution)/shard_map/ppermute | solution.py:15
  15.1 6.7 %copy-start.6 = (bf16[24,48,512]{2,1,0:T(8,128)(2,1)S(1)}, bf16[24,48,512]{2,1,0:T(8,128)(2,1)}, u32[]{:S(2)}) copy-start(bf16[24,48,512]{2,1,0:T(8,128)(2,1)} %param.6) | copy-start | bytes 3538948
  17.7 7.6 %collective-permute-start.1 = (bf16[27,6,512]{2,1,0:T(8,128)(2,1)S(1)}, bf16[27,6,512]{2,1,0:T(8,128)(2,1)S(1)}, u32[]{:S(2)}, u32[]{:S(2)}) collective-permute-start(bf16[27,6,512]{2,1,0:T(8,128)(2,1)S(1)} %slice.52), channel_id=1, source_target_pairs={{0,15},{1,0},{2,1},{3,2},{4,3},{5,4},{6,5},{7,6},{8,7},{9,8},{10,9... | collective-permute-start | bytes 497672 | tf_op jit(solution)/shard_map/ppermute | solution.py:15
  21.9 52.1 %collective-permute-start.3 = (bf16[27,6,512]{2,1,0:T(8,128)(2,1)S(1)}, bf16[27,6,512]{2,1,0:T(8,128)(2,1)}, u32[]{:S(2)}, u32[]{:S(2)}) collective-permute-start(bf16[27,6,512]{2,1,0:T(8,128)(2,1)S(1)} %slice.55), channel_id=1, source_target_pairs={{0,15},{1,0},{2,1},{3,2},{4,3},{5,4},{6,5},{7,6},{8,7},{9,8},{10,9... | collective-permute-start | bytes 497672 | tf_op jit(solution)/shard_map/ppermute | solution.py:15
  30.8 2.8 copy-start.1
  38.7 3.9 %copy-start.13 = (f32[512]{0:T(512)S(1)}, f32[512]{0:T(512)}, u32[]{:S(2)}) copy-start(f32[512]{0:T(512)} %param.7) | copy-start | bytes 6148
  82.3 1.0 copy-start.11
  92.5 4.9 %copy-start.12 = (pred[16,72,72]{1,2,0:T(8,128)(4,1)S(1)}, pred[16,72,72]{1,2,0:T(8,128)(4,1)}, u32[]{:S(2)}) copy-start(pred[16,72,72]{1,2,0:T(8,128)(4,1)} %broadcast_compare_fusion) | copy-start | bytes 248836
  97.5 5.3 %copy-start.4 = (bf16[16,72,16,32]{1,0,3,2:T(8,128)(2,1)S(1)}, bf16[16,72,16,32]{1,0,3,2:T(8,128)(2,1)}, u32[]{:S(2)}) copy-start(bf16[16,72,16,32]{1,0,3,2:T(8,128)(2,1)} %reshape.112) | copy-start | bytes 3538948
  97.5 5.3 %copy-start.5 = (bf16[16,72,1,16,32]{1,0,4,3,2:T(8,128)(2,1)S(1)}, bf16[16,72,1,16,32]{1,0,4,3,2:T(8,128)(2,1)}, u32[]{:S(2)}) copy-start(bf16[16,72,1,16,32]{1,0,4,3,2:T(8,128)(2,1)} %get-tuple-element.9) | copy-start | bytes 3538948
  102.8 6.6 %copy-start.14 = (f32[16,16,72,72]{2,3,1,0:T(8,128)S(1)}, f32[16,16,72,72]{2,3,1,0:T(8,128)}, u32[]{:S(2)}) copy-start(f32[16,16,72,72]{2,3,1,0:T(8,128)} %get-tuple-element.13) | copy-start | bytes 15925252
  146.1 8.4 %copy-start.2 = (f32[4,6,4,12,512]{4,3,2,1,0:T(8,128)S(1)}, f32[4,6,4,12,512]{4,3,2,1,0:T(8,128)}, u32[]{:S(2)}) copy-start(f32[4,6,4,12,512]{4,3,2,1,0:T(8,128)} %reshape.117) | copy-start | bytes 7077892
  154.5 1.6 copy-start.8
  163.8 3.6 copy-start.9
  163.8 3.6 copy-start.10
  200.9 6.0 %copy-start.3 = (f32[1152,512]{1,0:T(8,128)S(1)}, f32[1152,512]{1,0:T(8,128)}, u32[]{:S(2)}) copy-start(f32[1152,512]{1,0:T(8,128)} %reshape.116) | copy-start | bytes 7077892
  220.9 80.5 %copy-start.7 = (bf16[24,48,512]{2,1,0:T(8,128)(2,1)S(1)}, bf16[24,48,512]{2,1,0:T(8,128)(2,1)}, u32[]{:S(2)}) copy-start(bf16[24,48,512]{2,1,0:T(8,128)(2,1)} %param.6) | copy-start | bytes 3538948
  222.0 13.0 %collective-permute-start.4 = (f32[24,6,512]{2,1,0:T(8,128)S(1)}, f32[24,6,512]{2,1,0:T(8,128)S(1)}, u32[]{:S(2)}, u32[]{:S(2)}) collective-permute-start(f32[24,6,512]{2,1,0:T(8,128)S(1)} %slice.57), channel_id=1, source_target_pairs={{0,1},{1,2},{2,3},{3,4},{4,5},{5,6},{6,7},{7,8},{8,9},{9,10},{10,1... | collective-permute-start | bytes 884744 | tf_op jit(solution)/shard_map/ppermute | solution.py:15
  236.1 65.3 %collective-permute-start.5 = (f32[3,48,512]{2,1,0:T(8,128)S(1)}, f32[3,48,512]{2,1,0:T(8,128)}, u32[]{:S(2)}, u32[]{:S(2)}) collective-permute-start(f32[3,48,512]{2,1,0:T(8,128)S(1)} %pad_maximum_fusion.4), channel_id=1, source_target_pairs={{0,16},{16,32},{32,48},{48,64},{64,80},{80,96},{96,112},{112,0},{1... | collective-permute-start | bytes 884744 | tf_op jit(solution)/shard_map/ppermute | solution.py:15
Sparse Core Ops, SparseCore 0:
  201.0 158.3 all-reduce.5
where the time goes:
time: 374 us; the launch traced here: 369 us
  local copies, waits for them, and re-layouts  102 us (27%)
  matrix products  79.8 us (21%)
  waiting for transfers between devices  69.9 us (19%)
  blocking collectives  64.5 us (17%)
  other arithmetic  26.6 us (7%)
  between operations  14.5 us (4%)
  starting transfers between devices  11.8 us (3%)
    unnamed x1, blocking collectives  64.5 us
    unnamed x2, waiting for transfers between devices  55 us
    dot_general x1, matrix products, window_grads(): jnp.einsum('bhqk,bkhd->bqhd', grad_score, key_heads, preferred_element_ty...  17 us
    dot_general x1, matrix products, window_grads(): jnp.einsum('bhqk,bqhd->bkhd', grad_score, query, preferred_element_type=j...  16.5 us
    ppermute x6, waiting for transfers between devices, shifted(): lax.ppermute(shard, axis, [(i, (i + by) % peers) for i in range(peers)])  15 us
    reshape x1, local copies, waits for them, and re-layouts, window_grads(): qkv_all = qkv_all.reshape(n_windows, win_span, 3, HEADS, head_size)  13.6 us
    convert_element_type x3, local copies, waits for them, and re-layouts, window_grads(): win_in.astype(jnp.float32).reshape(n_windows * win_span, channels)  11.9 us
    ppermute x6, starting transfers between devices, shifted(): lax.ppermute(shard, axis, [(i, (i + by) % peers) for i in range(peers)])  11.7 us
  transfers between devices with their start and end apart: 7, of which 4 were waited for; matrix products, arithmetic and copies ran while one was open for 21% of the time, Pallas kernels for 0%

commit v1 on v0

v1 whole, which is shorter than its diff:
```python
import functools
import math

import jax
import jax.numpy as jnp
import numpy as np
from jax import lax
from jax.experimental import pallas as pl
from jax.experimental.pallas import tpu as pltpu
from jax.sharding import PartitionSpec as P

C = 512
HEADS = 16
HEAD = C // HEADS
WIN_LAT = 6
WIN_LON = 12
SPAN = WIN_LAT * WIN_LON
ROWS = 24
COLS = 48
BANDS = ROWS // WIN_LAT
PER_BAND = COLS // WIN_LON
BAND = WIN_LAT * COLS
TOKENS = ROWS * COLS
HALF_LAT = WIN_LAT // 2
HALF_LON = WIN_LON // 2
SIDE = 48
GROUP = 128 // HEAD
F32 = jnp.float32
BF16 = jnp.bfloat16


def window_order():
    perm = np.zeros((BAND, BAND + SIDE), np.float32)
    for b in range(PER_BAND):
        for r in range(WIN_LAT):
            for c in range(WIN_LON):
                col = WIN_LON * b + HALF_LON + c
                src = r * COLS + col if col < COLS else BAND + r * HALF_LON + col - COLS
                perm[b * SPAN + r * WIN_LON + c, src] = 1.0
    return perm


def nn(a, b):
    return lax.dot_general(a, b, (((1,), (0,)), ((), ())), preferred_element_type=F32)


def nt(a, b):
    return lax.dot_general(a, b, (((1,), (1,)), ((), ())), preferred_element_type=F32)


def tn(a, b):
    return lax.dot_general(a, b, (((0,), (0,)), ((), ())), preferred_element_type=F32)


def local_kernel(
    own_in, own_cot, low_in, low_cot, side_in, side_cot, gain, wqkv, wproj, perm, perm_t, bias,
    out_ref, out_low, out_side, gqkv_ref, gproj_ref,
    ext_in, ext_cot, normed, inv_std, scaled, cot_win, qkv, grad_att, att, grad_all, out_ext,
):
    ext_in[0:TOKENS] = own_in[...]
    ext_cot[0:TOKENS] = own_cot[...]
    ext_in[TOKENS:] = low_in[...]
    ext_cot[TOKENS:] = low_cot[...]

    def forward(a, carry):
        src = pl.ds(pl.multiple_of(a * BAND + HALF_LAT * COLS, 16), BAND)
        dst = pl.ds(pl.multiple_of(a * BAND, 16), BAND)
        side = pl.ds(pl.multiple_of(a * SIDE, 16), SIDE)
        x = nn(perm[...], jnp.concatenate([ext_in[src], side_in[side]], axis=0))
        cot = nn(perm[...], jnp.concatenate([ext_cot[src], side_cot[side]], axis=0)).astype(BF16)
        center = x - jnp.mean(x, axis=-1, keepdims=True)
        inv = lax.rsqrt(jnp.mean(center * center, axis=-1, keepdims=True) + 1e-05)
        norm = center * inv
        normed[dst] = norm
        inv_std[dst] = jnp.broadcast_to(inv, (BAND, 128))
        sc = (norm * gain[...]).astype(BF16)
        scaled[dst] = sc
        cot_win[dst] = cot
        qkv[dst] = nn(sc, wqkv[...]).astype(BF16).astype(F32)
        grad_att[dst] = nt(cot, wproj[...]).astype(BF16).astype(F32)
        return carry

    lax.fori_loop(0, BANDS, forward, 0)

    lane = lax.broadcasted_iota(jnp.int32, (1, 128), 1) // HEAD
    masks = [(lane == j).astype(F32) for j in range(GROUP)]

    def stacked(x):
        return jnp.concatenate([x * m for m in masks], axis=0).astype(BF16)

    def by_head(x):
        x = x.reshape(GROUP, SPAN, 128)
        y = x[GROUP - 1]
        for j in range(GROUP - 2, -1, -1):
            y = jnp.where(lane == j, x[j], y)
        return y

    scale = HEAD ** (-0.5)

    def attention(w, carry):
        rows = pl.ds(pl.multiple_of(w * SPAN, 8), SPAN)
        edge = jnp.where(w >= (BANDS - 1) * PER_BAND, 1.0, 0.0)
        shut = bias[...] * edge
        for g in range(C // 128):
            cols = slice(g * 128, (g + 1) * 128)
            q = qkv[rows, g * 128 : (g + 1) * 128].astype(BF16)
            k_st = stacked(qkv[rows, C + g * 128 : C + (g + 1) * 128])
            v_st = stacked(qkv[rows, 2 * C + g * 128 : 2 * C + (g + 1) * 128])
            da = grad_att[rows, cols].astype(BF16)
            s = nt(k_st, q).reshape(GROUP, SPAN, SPAN) * scale + shut
            ex = jnp.exp(s - jnp.max(s, axis=1, keepdims=True))
            prob = ex * (1.0 / jnp.sum(ex, axis=1, keepdims=True))
            gp = nt(v_st, da).reshape(GROUP, SPAN, SPAN)
            inner = jnp.sum(prob * gp, axis=1, keepdims=True)
            gs = (prob * (gp - inner) * scale).reshape(GROUP * SPAN, SPAN).astype(BF16)
            pb = prob.reshape(GROUP * SPAN, SPAN).astype(BF16)
            att[rows, cols] = tn(pb, v_st)
            grad_all[rows, g * 128 : (g + 1) * 128] = tn(gs, k_st)
            grad_all[rows, C + g * 128 : C + (g + 1) * 128] = by_head(nn(gs, q))
            grad_all[rows, 2 * C + g * 128 : 2 * C + (g + 1) * 128] = by_head(nn(pb, da))
        return carry

    lax.fori_loop(0, BANDS * PER_BAND, attention, 0)

    gproj_ref[...] = tn(att[...].astype(BF16), cot_win[...])
    for j in range(3):
        cols = slice(j * C, (j + 1) * C)
        gqkv_ref[:, cols] = tn(scaled[...], grad_all[:, cols].astype(BF16))

    def backward(a, carry):
        dst = pl.ds(pl.multiple_of(a * BAND, 16), BAND)
        gn = nt(grad_all[dst].astype(BF16), wqkv[...]) * gain[...]
        norm = normed[dst]
        branch = inv_std[dst][:, 0:1] * (
            gn
            - jnp.mean(gn, axis=-1, keepdims=True)
            - norm * jnp.mean(gn * norm, axis=-1, keepdims=True)
        )
        out = (cot_win[dst].astype(F32) + branch).astype(BF16)
        slab = nn(perm_t[...], out).astype(BF16)
        out_ext[pl.ds(pl.multiple_of(a * BAND, 16), BAND)] = slab[:BAND]
        out_side[pl.ds(pl.multiple_of(a * SIDE, 16), SIDE)] = slab[BAND:]
        return carry

    lax.fori_loop(0, BANDS, backward, 0)
    lead = HALF_LAT * COLS
    out_ref[0:lead] = jnp.zeros((lead, C), BF16)
    out_ref[lead:] = out_ext[0 : TOKENS - lead]
    out_low[...] = out_ext[TOKENS - lead :]


def local_grads(*args):
    vmem = pl.BlockSpec(memory_space=pltpu.VMEM)
    lead = HALF_LAT * COLS
    return pl.pallas_call(
        local_kernel,
        out_shape=(
            jax.ShapeDtypeStruct((TOKENS, C), BF16),
            jax.ShapeDtypeStruct((lead, C), BF16),
            jax.ShapeDtypeStruct((BANDS * SIDE, C), BF16),
            jax.ShapeDtypeStruct((C, 3 * C), F32),
            jax.ShapeDtypeStruct((C, C), F32),
        ),
        in_specs=[vmem] * 12,
        out_specs=(vmem,) * 5,
        scratch_shapes=[
            pltpu.VMEM((TOKENS + lead, C), BF16),
            pltpu.VMEM((TOKENS + lead, C), BF16),
            pltpu.VMEM((TOKENS, C), F32),
            pltpu.VMEM((TOKENS, 128), F32),
            pltpu.VMEM((TOKENS, C), BF16),
            pltpu.VMEM((TOKENS, C), BF16),
            pltpu.VMEM((TOKENS, 3 * C), F32),
            pltpu.VMEM((TOKENS, C), F32),
            pltpu.VMEM((TOKENS, C), F32),
            pltpu.VMEM((TOKENS, 3 * C), F32),
            pltpu.VMEM((TOKENS, C), BF16),
        ],
        compiler_params=pltpu.CompilerParams(vmem_limit_bytes=60 * 1024 * 1024),
        name="window_grads",
    )(*args)


def shifted(shard, axis, by):
    peers = lax.axis_size(axis)
    return lax.ppermute(shard, axis, [(i, (i + by) % peers) for i in range(peers)])


def on_device(activations, cotangent, norm_gain, qkv_weight, proj_weight):
    both = jnp.stack([activations, cotangent])
    low = shifted(both[:, :HALF_LAT], "lat", -1)
    edge = jnp.concatenate([both[:, HALF_LAT:, :HALF_LON], low[:, :, :HALF_LON]], axis=1)
    side = shifted(edge, "lon", -1)
    side = side.reshape(2, BANDS, WIN_LAT * HALF_LON, C)
    side = jnp.pad(side, ((0, 0), (0, 0), (0, SIDE - WIN_LAT * HALF_LON), (0, 0)))
    side = side.reshape(2, BANDS * SIDE, C)
    low = low.reshape(2, HALF_LAT * COLS, C)
    perm = window_order()
    half = np.arange(SPAN) >= HALF_LAT * WIN_LON
    shut = np.where(half[:, None] == half[None, :], 0.0, -1e30).astype(np.float32)
    last = lax.axis_index("lat") == lax.axis_size("lat") - 1
    bias = jnp.where(last, jnp.asarray(shut), 0.0)
    out, out_low, out_side, gqkv, gproj = local_grads(
        activations.reshape(TOKENS, C),
        cotangent.reshape(TOKENS, C),
        low[0], low[1], side[0], side[1],
        norm_gain.reshape(1, C),
        qkv_weight,
        proj_weight,
        jnp.asarray(perm, BF16),
        jnp.asarray(perm.T, BF16),
        bias,
    )
    out_side = out_side.reshape(BANDS, SIDE, C)[:, : WIN_LAT * HALF_LON].reshape(ROWS, HALF_LON, C)
    left = shifted(out_side, "lon", 1)
    low_rows = out_low.reshape(HALF_LAT, COLS, C)[:, HALF_LON:]
    low_rows = jnp.concatenate([left[ROWS - HALF_LAT :], low_rows], axis=1)
    top = shifted(low_rows, "lat", 1)
    rest = out.reshape(ROWS, COLS, C)[HALF_LAT:, HALF_LON:]
    rest = jnp.concatenate([left[: ROWS - HALF_LAT], rest], axis=1)
    grad_input = jnp.concatenate([top, rest], axis=0)
    token_scale = 1.0 / math.sqrt(TOKENS * lax.axis_size("lat") * lax.axis_size("lon"))
    gqkv = lax.psum_scatter(gqkv, ("lat", "lon"), scatter_dimension=0, tiled=True)
    gproj = lax.psum_scatter(gproj, ("lat", "lon"), scatter_dimension=0, tiled=True)
    gqkv = gqkv * token_scale
    me = lax.axis_index("lat") * lax.axis_size("lon") + lax.axis_index("lon")
    share = gqkv.shape[0]
    w_rows = lax.dynamic_slice_in_dim(qkv_weight, me * share, share, 0).astype(F32)
    gain_rows = lax.dynamic_slice_in_dim(norm_gain, me * share, share, 0)
    ggain = jnp.sum(gqkv * w_rows, axis=1) / gain_rows
    return grad_input, gqkv, gproj * token_scale, ggain


def solution(mesh):
    return jax.shard_map(
        on_device,
        mesh=mesh,
        in_specs=(P("lat", "lon", None), P("lat", "lon", None), P(), P(), P()),
        out_specs=(
            P("lat", "lon", None),
            P(("lat", "lon"), None),
            P(("lat", "lon"), None),
            P(("lat", "lon")),
        ),
        check_vma=False,
    )
```

time: 374 us -> 241 us (0.64); the launches traced: 369 us -> 240 us
  local copies, waits for them, and re-layouts: 102 us -> 4.48 us
  waiting for transfers between devices: 69.9 us -> 163 us
  matrix products: 79.8 us -> 0 us
  blocking collectives: 64.5 us -> 0 us
  Pallas kernels: 0 us -> 41.7 us
  other arithmetic: 26.6 us -> 7.52 us
    unnamed x2, waiting for transfers between devices: 55 us -> 137 us
    dot_general x11 -> x0, matrix products: 79.8 us -> none  [the longest x1 17 us: window_grads(): jnp.einsum('bhqk,bkhd->bqhd', grad_score, key_heads, preferred_element_ty...]
    unnamed x1 -> x0, blocking collectives: 64.5 us -> none
    pallas_call x0 -> x1, Pallas kernels: none -> 41.7 us  [local_grads(): pl.pallas_call(local_kernel, out_shape=(jax.ShapeDtypeStruct((TOKENS, C),...]
    reshape x6 -> x1, local copies, waits for them, and re-layouts: 40 us -> 0.06 us  [on_device(): out_side.reshape(BANDS, SIDE, C)[:, :WIN_LAT * HALF_LON]]
    convert_element_type x8 -> x0, local copies, waits for them, and re-layouts: 25.8 us -> none  [the longest x3 11.9 us: window_grads(): win_in.astype(jnp.float32).reshape(n_windows * win_span, channels)]
    another operation x3 -> x0, local copies, waits for them, and re-layouts: 16.2 us -> none  [the longest x1 9.94 us: window_grads(): jnp.stack([grad_query, grad_key, grad_val], axis=2)]
    ppermute x6 -> x4, waiting for transfers between devices: 15 us -> 26 us  [shifted(): lax.ppermute(shard, axis, [(i, (i + by) % peers) for i in range(peers)])]
  transfers between devices with their start and end apart: 7 -> 5, of which waited for: 4 -> 5; matrix products, arithmetic and copies ran while one was open for 21% -> 1% of each run, Pallas kernels for 0% -> 0%
where the time goes in v1:
time: 241 us; the launch traced here: 240 us
  waiting for transfers between devices  163 us (68%)
  Pallas kernels  41.7 us (17%)
  between operations  14.2 us (6%)
  starting transfers between devices  9.12 us (4%)
  other arithmetic  7.52 us (3%)
  local copies, waits for them, and re-layouts  4.48 us (2%)
    unnamed x2, waiting for transfers between devices  137 us
    pallas_call x1, Pallas kernels, local_grads(): pl.pallas_call(local_kernel, out_shape=(jax.ShapeDtypeStruct((TOKENS, C),...  41.7 us
    ppermute x4, waiting for transfers between devices, shifted(): lax.ppermute(shard, axis, [(i, (i + by) % peers) for i in range(peers)])  26 us
    ppermute x4, starting transfers between devices, shifted(): lax.ppermute(shard, axis, [(i, (i + by) % peers) for i in range(peers)])  9.08 us
  transfers between devices with their start and end apart: 5, of which 5 were waited for; matrix products, arithmetic and copies ran while one was open for 1% of the time, Pallas kernels for 0%

profile of v1, /device:TPU:0, one launch (start us, length us, event | category | flops | bytes accessed | tf_op | source)
XLA Modules:
  0.0 240.4 jit_solution(12030444821132477020)
XLA Ops:
  7.2 1.2 pad_maximum_fusion.1
  8.4 5.1 %collective-permute-start = (bf16[2,3,48,512]{3,2,1,0:T(8,128)(2,1)S(1)}, bf16[2,3,48,512]{3,2,1,0:T(8,128)(2,1)S(1)}, u32[]{:S(2)}, u32[]{:S(2)}) collective-permute-start(bf16[2,3,48,512]{3,2,1,0:T(8,128)(2,1)S(1)} %pad_maximum_fusion.1), channel_id=1, source_target_pairs={{0,112},{16,0},{32,16},{48,32},{64,48},{80,64},{96,80},{112,96},{1... | collective-permute-start | bytes 884744 | tf_op jit(solution)/shard_map/ppermute | solution.py:186
  13.5 6.3 %collective-permute-done = bf16[2,3,48,512]{3,2,1,0:T(8,128)(2,1)S(1)} collective-permute-done((bf16[2,3,48,512]{3,2,1,0:T(8,128)(2,1)S(1)}, bf16[2,3,48,512]{3,2,1,0:T(8,128)(2,1)S(1)}, u32[]{:S(2)}, u32[]{:S(2)}) %collective-permute-start) | collective-permute-done | bytes 294944 | tf_op jit(solution)/shard_map/ppermute | solution.py:186
  19.8 3.8 %collective-permute-start.1 = (bf16[2,24,6,512]{3,2,1,0:T(8,128)(2,1)S(1)}, bf16[2,24,6,512]{3,2,1,0:T(8,128)(2,1)S(1)}, u32[]{:S(2)}, u32[]{:S(2)}) collective-permute-start(bf16[2,24,6,512]{3,2,1,0:T(8,128)(2,1)S(1)} %fusion), channel_id=1, source_target_pairs={{0,15},{1,0},{2,1},{3,2},{4,3},{5,4},{6,5},{7,6},{8,7},{9,8},{10,9... | collective-permute-start | bytes 884744 | tf_op jit(solution)/shard_map/ppermute | solution.py:186
  23.7 0.6 broadcast_select_fusion.bias
  24.3 0.7 fusion.1
  25.0 4.0 %collective-permute-done.1 = bf16[2,24,6,512]{3,2,1,0:T(8,128)(2,1)S(1)} collective-permute-done((bf16[2,24,6,512]{3,2,1,0:T(8,128)(2,1)S(1)}, bf16[2,24,6,512]{3,2,1,0:T(8,128)(2,1)S(1)}, u32[]{:S(2)}, u32[]{:S(2)}) %collective-permute-start.1) | collective-permute-done | bytes 294944 | tf_op jit(solution)/shard_map/ppermute | solution.py:186
  29.0 0.3 copy.14
  29.3 0.6 pad_slice_fusion
  29.9 0.7 copy.15
  30.6 0.7 copy.16
  31.3 41.7 %window_grads.1 = (bf16[1152,512]{1,0:T(8,128)(2,1)}, bf16[144,512]{1,0:T(8,128)(2,1)}, bf16[192,512]{1,0:T(8,128)(2,1)}, f32[512,1536]{1,0:T(8,128)}, f32[512,512]{1,0:T(8,128)}) custom-call(bf16[1152,512]{1,0:T(8,128)(2,1)} %bitcast.14, bf16[1152,512]{1,0:T(8,128)(2,1)} %bitcast.17, bf16[144,512]{1,0:T(8,128)(2,1)} %bitcast.24, bf16[144,512]{1,0:T(8,128)(2,1)} %bitcast.23, ...), custom_call_target="tpu_custom_call" | custom-call | tf_op jit(solution)/shard_map/window_grads/pallas_call | solution.py:155
  73.0 0.9 copy-done.4
  73.9 0.1 reshape.47
  74.0 0.1 collective-permute-start.2
  74.1 8.8 %collective-permute-done.2 = bf16[24,6,512]{2,1,0:T(8,128)(2,1)S(1)} collective-permute-done((bf16[24,6,512]{2,1,0:T(8,128)(2,1)S(1)}, bf16[24,6,512]{2,1,0:T(8,128)(2,1)S(1)}, u32[]{:S(2)}, u32[]{:S(2)}) %collective-permute-start.2) | collective-permute-done | bytes 147488 | tf_op jit(solution)/shard_map/ppermute | solution.py:186
  82.9 0.1 collective-permute-start.3
  83.1 0.4 slice.59
  83.5 7.0 %collective-permute-done.3 = bf16[3,48,512]{2,1,0:T(8,128)(2,1)S(1)} collective-permute-done((bf16[3,48,512]{2,1,0:T(8,128)(2,1)S(1)}, bf16[3,48,512]{2,1,0:T(8,128)(2,1)S(1)}, u32[]{:S(2)}, u32[]{:S(2)}) %collective-permute-start.3) | collective-permute-done | bytes 147488 | tf_op jit(solution)/shard_map/ppermute | solution.py:186
  90.5 1.5 maximum_maximum_fusion
  92.0 137.4 %all-reduce.6.cloned.1.call-done = (f32[512,1536]{1,0:T(8,128)}, f32[512,512]{1,0:T(8,128)}) async-done(((f32[512,1536]{1,0:T(8,128)}, f32[512,512]{1,0:T(8,128)}), (f32[512,1536]{1,0:T(8,128)}, f32[512,512]{1,0:T(8,128)})) %all-reduce.6.cloned.1.call-update) | async-done | bytes 4194320
  229.4 1.3 dynamic-slice_multiply_fusion.1
  230.7 1.6 multiply_reduce_fusion
  232.3 1.3 dynamic-slice_divide_fusion
  (20 shorter events, 0.2 us)
Async XLA Ops:
  7.2 222.2 %all-reduce.6.cloned.1.call-start = ((), (), s32[]{:S(2)}) async-start(), calls=%async_computation | async-start | bytes 8388608
  7.2 12.6 %copy-start = (bf16[24,48,512]{2,1,0:T(8,128)(2,1)S(1)}, bf16[24,48,512]{2,1,0:T(8,128)(2,1)}, u32[]{:S(2)}) copy-start(bf16[24,48,512]{2,1,0:T(8,128)(2,1)} %param.8) | copy-start | bytes 3538948
  7.2 12.6 %copy-start.1 = (bf16[24,48,512]{2,1,0:T(8,128)(2,1)S(1)}, bf16[24,48,512]{2,1,0:T(8,128)(2,1)}, u32[]{:S(2)}) copy-start(bf16[24,48,512]{2,1,0:T(8,128)(2,1)} %param.9) | copy-start | bytes 3538948
  8.4 11.4 %collective-permute-start = (bf16[2,3,48,512]{3,2,1,0:T(8,128)(2,1)S(1)}, bf16[2,3,48,512]{3,2,1,0:T(8,128)(2,1)S(1)}, u32[]{:S(2)}, u32[]{:S(2)}) collective-permute-start(bf16[2,3,48,512]{3,2,1,0:T(8,128)(2,1)S(1)} %pad_maximum_fusion.1), channel_id=1, source_target_pairs={{0,112},{16,0},{32,16},{48,32},{64,48},{80,64},{96,80},{112,96},{1... | collective-permute-start | bytes 884744 | tf_op jit(solution)/shard_map/ppermute | solution.py:186
  19.8 3.9 %copy-start.5 = (f32[72,72]{1,0:T(8,128)S(1)}, f32[72,72]{1,0:T(8,128)}, u32[]{:S(2)}) copy-start(f32[72,72]{1,0:T(8,128)} %constant.32.clone) | copy-start | bytes 62212
  19.8 9.1 %collective-permute-start.1 = (bf16[2,24,6,512]{3,2,1,0:T(8,128)(2,1)S(1)}, bf16[2,24,6,512]{3,2,1,0:T(8,128)(2,1)S(1)}, u32[]{:S(2)}, u32[]{:S(2)}) collective-permute-start(bf16[2,24,6,512]{3,2,1,0:T(8,128)(2,1)S(1)} %fusion), channel_id=1, source_target_pairs={{0,15},{1,0},{2,1},{3,2},{4,3},{5,4},{6,5},{7,6},{8,7},{9,8},{10,9... | collective-permute-start | bytes 884744 | tf_op jit(solution)/shard_map/ppermute | solution.py:186
  72.9 0.9 copy-start.4
  73.0 1.1 copy-start.3
  73.0 10.1 %copy-start.2 = (bf16[1152,512]{1,0:T(8,128)(2,1)S(1)}, bf16[1152,512]{1,0:T(8,128)(2,1)}, u32[]{:S(2)}) copy-start(bf16[1152,512]{1,0:T(8,128)(2,1)} %get-tuple-element.11) | copy-start | bytes 3538948
  74.0 8.9 %collective-permute-start.2 = (bf16[24,6,512]{2,1,0:T(8,128)(2,1)S(1)}, bf16[24,6,512]{2,1,0:T(8,128)(2,1)S(1)}, u32[]{:S(2)}, u32[]{:S(2)}) collective-permute-start(bf16[24,6,512]{2,1,0:T(8,128)(2,1)S(1)} %reshape.47), channel_id=1, source_target_pairs={{0,1},{1,2},{2,3},{3,4},{4,5},{5,6},{6,7},{7,8},{8,9},{9,10},{10,1... | collective-permute-start | bytes 442376 | tf_op jit(solution)/shard_map/ppermute | solution.py:186
  82.9 7.5 %collective-permute-start.3 = (bf16[3,48,512]{2,1,0:T(8,128)(2,1)S(1)}, bf16[3,48,512]{2,1,0:T(8,128)(2,1)S(1)}, u32[]{:S(2)}, u32[]{:S(2)}) collective-permute-start(bf16[3,48,512]{2,1,0:T(8,128)(2,1)S(1)} %pad_maximum_fusion.2), channel_id=1, source_target_pairs={{0,16},{16,32},{32,48},{48,64},{64,80},{80,96},{96,112},{112,0},{1... | collective-permute-start | bytes 442376 | tf_op jit(solution)/shard_map/ppermute | solution.py:186
Sparse Core Ops, SparseCore 0:
  73.1 156.2 all-reduce.5

commit v2 on v1

v2 whole, which is shorter than its diff:
```python
import math

import jax
import jax.numpy as jnp
import numpy as np
from jax import lax
from jax.experimental import pallas as pl
from jax.experimental.pallas import tpu as pltpu
from jax.sharding import PartitionSpec as P

C = 512
HEADS = 16
HEAD = C // HEADS
WIN_LAT = 6
WIN_LON = 12
SPAN = WIN_LAT * WIN_LON
ROWS = 24
COLS = 48
BANDS = ROWS // WIN_LAT
PER_BAND = COLS // WIN_LON
BAND = WIN_LAT * COLS
TOKENS = ROWS * COLS
HALF_LAT = WIN_LAT // 2
HALF_LON = WIN_LON // 2
SIDE = 48
GROUP = 128 // HEAD
F32 = jnp.float32
BF16 = jnp.bfloat16


def window_order():
    perm = np.zeros((BAND, BAND + SIDE), np.float32)
    for b in range(PER_BAND):
        for r in range(WIN_LAT):
            for c in range(WIN_LON):
                col = WIN_LON * b + HALF_LON + c
                src = r * COLS + col if col < COLS else BAND + r * HALF_LON + col - COLS
                perm[b * SPAN + r * WIN_LON + c, src] = 1.0
    return perm


def nn(a, b):
    return lax.dot_general(a, b, (((1,), (0,)), ((), ())), preferred_element_type=F32)


def nt(a, b):
    return lax.dot_general(a, b, (((1,), (1,)), ((), ())), preferred_element_type=F32)


def tn(a, b):
    return lax.dot_general(a, b, (((0,), (0,)), ((), ())), preferred_element_type=F32)


PARTS = ((0, 256, "zyx"), (256, 128, "xzy"), (384, 128, "yxz"))
MESH = pl.DeviceIdType.MESH
LEAD = HALF_LAT * COLS
PAIR = 2 * SPAN


def place():
    lat, lon = lax.axis_index("lat"), lax.axis_index("lon")
    spot = {"z": lat // 2, "x": (lon // 2) % 2 * 2 + lat % 2, "y": lon // 4}
    return lat, lon, spot, lon % 2


def device_at(spot, core):
    return (spot["z"] * 2 + spot["x"] % 2, spot["y"] * 4 + spot["x"] // 2 * 2 + core)


def along(spot, axis, by):
    return {**spot, axis: (spot[axis] + by) % 4}


def chip_at(at):
    return at["z"] * 16 + at["x"] % 2 * 8 + at["y"] * 2 + at["x"] // 2


def sublayer_kernel(
    own_in, own_cot, gain, wqkv_hbm, wproj_hbm, perm, perm_t, spread,
    out_ref, gqkv_ref, gproj_ref, ggain_ref,
    ext, side, side_out, corner, corner_out, wqkv, wproj,
    normed, inv_std, scaled, cot_win, scaled_t, att_t, qkv, grad_att, att, grad_all,
    out_ext, back_side, top, left, back_corner, grads, mine, theirs, got0,
    *rest,
):
    buffers, (local, send, recv) = rest[:-3], rest[-3:]
    loads = [
        pltpu.make_async_copy(own_in, ext.at[0, pl.ds(0, TOKENS)], local.at[0]),
        pltpu.make_async_copy(own_cot, ext.at[1, pl.ds(0, TOKENS)], local.at[1]),
        pltpu.make_async_copy(wqkv_hbm, wqkv, local.at[2]),
        pltpu.make_async_copy(wproj_hbm, wproj, local.at[3]),
    ]
    for load in loads:
        load.start()

    lat, lon, spot, core = place()
    lats, lons = lax.axis_size("lat"), lax.axis_size("lon")
    sibling = device_at(spot, 1 - core)
    down, up = (lat + 1) % lats, (lat + lats - 1) % lats
    east, west = (lon + 1) % lons, (lon + lons - 1) % lons
    peers = [sibling, (down, lon), (up, lon), (lat, east), (lat, west), (down, east), (up, west)]
    for axis in "xyz":
        peers += [device_at(along(spot, axis, k), core) for k in (1, 2, 3)]
    barrier = pltpu.get_barrier_semaphore()
    for peer in peers:
        pl.semaphore_signal(barrier, inc=1, device_id=peer, device_id_type=MESH)

    count = [0]

    def remote(src, dst, peer):
        i = count[0]
        count[0] += 1
        copy = pltpu.make_async_remote_copy(
            src_ref=src, dst_ref=dst, send_sem=send.at[i], recv_sem=recv.at[i],
            device_id=peer, device_id_type=MESH,
        )
        copy.start()
        return copy

    loads[0].wait()
    loads[1].wait()
    for i in range(2):
        for a in range(BANDS):
            rows = BAND if a < BANDS - 1 else BAND - LEAD
            start = LEAD + a * BAND
            side_out[i, a * SIDE : (a + 1) * SIDE] = tn(
                spread[0:rows], ext[i, start : start + rows]
            ).astype(BF16)
        corner_out[i] = tn(spread[BAND - LEAD :], ext[i, 0:LEAD]).astype(BF16)
    pl.semaphore_wait(barrier, len(peers))
    halo = [
        remote(side_out, side, (lat, west)),
        remote(ext.at[:, pl.ds(0, LEAD)], ext.at[:, pl.ds(TOKENS, LEAD)], (up, lon)),
        remote(corner_out, corner, (up, west)),
    ]

    def forward(pieces):
        gathered = []
        for i in range(2):
            parts = []
            for a, half in pieces:
                start = LEAD + a * BAND
                src = ext[i, start : start + BAND]
                rows = perm[half * PAIR : (half + 1) * PAIR]
                if half == 0:
                    parts.append(nn(rows[:, :BAND], src))
                else:
                    edge = side[i, a * SIDE : (a + 1) * SIDE]
                    if a == BANDS - 1:
                        edge = (edge.astype(F32) + corner[i].astype(F32)).astype(BF16)
                    parts.append(nn(rows, jnp.concatenate([src, edge], axis=0)))
            gathered.append(jnp.concatenate(parts, axis=0))
        x, cot = gathered[0], gathered[1].astype(BF16)
        center = x - jnp.mean(x, axis=-1, keepdims=True)
        inv = lax.rsqrt(jnp.mean(center * center, axis=-1, keepdims=True) + 1e-05)
        norm = center * inv
        sc = (norm * gain[...]).astype(BF16)
        qkv_now = nn(sc, wqkv[...]).astype(BF16).astype(F32)
        att_now = nt(cot, wproj[...]).astype(BF16).astype(F32)
        for i, (a, half) in enumerate(pieces):
            dst = slice(a * BAND + half * PAIR, a * BAND + (half + 1) * PAIR)
            src = slice(i * PAIR, (i + 1) * PAIR)
            normed[dst] = norm[src]
            inv_std[dst] = jnp.broadcast_to(inv[src], (PAIR, 128))
            scaled[dst] = sc[src]
            cot_win[dst] = cot[src]
            qkv[dst] = qkv_now[src]
            grad_att[dst] = att_now[src]

    lane = lax.broadcasted_iota(jnp.int32, (1, 128), 1) // HEAD
    masks = [(lane == j).astype(F32) for j in range(GROUP)]
    key_half = lax.broadcasted_iota(jnp.int32, (SPAN, SPAN), 0) >= HALF_LAT * WIN_LON
    query_half = lax.broadcasted_iota(jnp.int32, (SPAN, SPAN), 1) >= HALF_LAT * WIN_LON
    parted = jnp.where(key_half == query_half, 0.0, -1e30)

    def stacked(x):
        return jnp.concatenate([x * m for m in masks], axis=0).astype(BF16)

    def by_head(x):
        x = x.reshape(GROUP, SPAN, 128)
        y = x[GROUP - 1]
        for j in range(GROUP - 2, -1, -1):
            y = jnp.where(lane == j, x[j], y)
        return y

    scale = HEAD ** (-0.5)

    def attention(w):
        rows = pl.ds(pl.multiple_of(w * SPAN, 8), SPAN)
        edge = jnp.where((lat == lats - 1) & (w >= (BANDS - 1) * PER_BAND), 1.0, 0.0)
        shut = parted * edge
        for g in range(C // 128):
            cols = slice(g * 128, (g + 1) * 128)
            q = qkv[rows, g * 128 : (g + 1) * 128].astype(BF16)
            k_st = stacked(qkv[rows, C + g * 128 : C + (g + 1) * 128])
            v_st = stacked(qkv[rows, 2 * C + g * 128 : 2 * C + (g + 1) * 128])
            da = grad_att[rows, cols].astype(BF16)
            s = nt(k_st, q).reshape(GROUP, SPAN, SPAN) * scale + shut
            ex = jnp.exp(s - jnp.max(s, axis=1, keepdims=True))
            prob = ex * (1.0 / jnp.sum(ex, axis=1, keepdims=True))
            gp = nt(v_st, da).reshape(GROUP, SPAN, SPAN)
            inner = jnp.sum(prob * gp, axis=1, keepdims=True)
            gs = (prob * (gp - inner) * scale).reshape(GROUP * SPAN, SPAN).astype(BF16)
            pb = prob.reshape(GROUP * SPAN, SPAN).astype(BF16)
            att[rows, cols] = tn(pb, v_st)
            grad_all[rows, g * 128 : (g + 1) * 128] = tn(gs, k_st)
            grad_all[rows, C + g * 128 : C + (g + 1) * 128] = by_head(nn(gs, q))
            grad_all[rows, 2 * C + g * 128 : 2 * C + (g + 1) * 128] = by_head(nn(pb, da))

    loads[2].wait()
    loads[3].wait()
    forward([(a, 0) for a in range(BANDS - 1)])

    def early(i, carry):
        attention(i // 2 * PER_BAND + i % 2)
        return carry

    lax.fori_loop(0, 2 * (BANDS - 1), early, 0)
    for copy in halo:
        copy.wait_recv()
    forward([(a, 1) for a in range(BANDS - 1)])
    forward([(BANDS - 1, 0), (BANDS - 1, 1)])

    def late(i, carry):
        attention(jnp.where(i < 6, i // 2 * PER_BAND + 2 + i % 2, i + 6))
        return carry

    lax.fori_loop(0, 2 * (BANDS + 1), late, 0)

    scaled_t[...] = scaled[...].T
    att_t[...] = att[...].astype(BF16).T
    upper = lax.broadcasted_iota(jnp.int32, (1, 8, 1), 1) < 4
    first_core = lax.broadcasted_iota(jnp.int32, (1, 8, 1), 1) * 0 + core == 0
    first = []
    for half in range(2):
        lo = half * 256
        lanes = slice(lo, lo + 256)
        for j in range(3):
            cols = slice(j * C + lo, j * C + lo + 256)
            grads[j] = nn(scaled_t[...], grad_all[:, cols].astype(BF16))
        grads[3] = nn(att_t[...], cot_win[:, lanes])

        def pack(i, carry):
            rows = pl.ds(pl.multiple_of(i * 64, 64), 64)
            chips = pl.ds(i * 8, 8)
            t = [grads[j, rows].reshape(8, 8, 256) for j in range(4)]
            turned = [pltpu.roll(x, 4, 1) for x in t]
            block = []
            for near, far in ((t, turned), (turned, t)):
                block.append(
                    jnp.concatenate(
                        [jnp.where(upper, near[j], far[j + 1]) for j in (0, 2)], axis=1
                    )
                )
            is_first = jnp.concatenate([first_core, first_core], axis=1)
            mine[chips, :, lanes] = jnp.where(is_first, block[0], block[1])
            theirs[chips, :, lanes] = jnp.where(is_first, block[1], block[0]).astype(BF16)
            return carry

        lax.fori_loop(0, 8, pack, 0)
        for start, width, _ in PARTS:
            if lo <= start < lo + 256:
                span = pl.ds(start, width)
                first.append(remote(theirs.at[:, :, span], got0.at[:, :, span], sibling))

    back = []

    def backward(a):
        dst = slice(a * BAND, (a + 1) * BAND)
        gn = nt(grad_all[dst].astype(BF16), wqkv[...]) * gain[...]
        norm = normed[dst]
        branch = inv_std[dst][:, 0:1] * (
            gn
            - jnp.mean(gn, axis=-1, keepdims=True)
            - norm * jnp.mean(gn * norm, axis=-1, keepdims=True)
        )
        done = (cot_win[dst].astype(F32) + branch).astype(BF16)
        slab = nn(perm_t[...], done).astype(BF16)
        out_ext[dst] = slab[:BAND]
        edge = slice(a * SIDE, (a + 1) * SIDE)
        back_side[edge] = slab[BAND:]
        edge = pl.ds(a * SIDE, SIDE)
        if a == BANDS - 1:
            back.append(remote(out_ext.at[pl.ds(TOKENS - LEAD, LEAD)], top, (down, lon)))
            back.append(remote(back_side.at[edge], back_corner, (down, east)))
        back.append(remote(back_side.at[edge], left.at[edge], (lat, east)))

    def summed0(p, chip):
        lo, width, _ = PARTS[p]
        lanes = slice(lo, lo + width)
        return mine[chip, :, lanes] + got0[chip, :, lanes].astype(F32)

    sent = [[] for _ in PARTS]

    def stage0(p):
        lo, width, order = PARTS[p]
        held = buffers[6 * p]
        first[p].wait_recv()

        def add(i, carry):
            at = dict(zip(order, (i // 16, i // 4 % 4, i % 4)))
            held[i // 16, i // 4 % 4, i % 4] = summed0(p, chip_at(at)).astype(BF16)
            return carry

        lax.fori_loop(0, 64, add, 0)
        for k in (1, 2, 3):
            peer = along(spot, order[0], k)
            sent[p].append(
                remote(held.at[peer[order[0]]], buffers[6 * p + 1].at[k - 1], device_at(peer, core))
            )

    def stage1(p):
        lo, width, order = PARTS[p]
        got, nxt, nxt_got = buffers[6 * p + 1 : 6 * p + 4]
        for copy in sent[p][-3:]:
            copy.wait_recv()

        def add(i, carry):
            at = dict(zip(order, (spot[order[0]], i // 4, i % 4)))
            total = summed0(p, chip_at(at))
            for k in range(3):
                total = total + got[k, i // 4, i % 4].astype(F32)
            nxt[i // 4, i % 4] = total
            return carry

        lax.fori_loop(0, 16, add, 0)
        for k in (1, 2, 3):
            peer = along(spot, order[1], k)
            sent[p].append(remote(nxt.at[peer[order[1]]], nxt_got.at[k - 1], device_at(peer, core)))

    def stage2(p):
        lo, width, order = PARTS[p]
        held, got, nxt, nxt_got = buffers[6 * p + 2 : 6 * p + 6]
        for copy in sent[p][-3:]:
            copy.wait_recv()
        nxt[...] = held[spot[order[1]]] + got[0] + got[1] + got[2]
        for k in (1, 2, 3):
            peer = along(spot, order[2], k)
            sent[p].append(remote(nxt.at[peer[order[2]]], nxt_got.at[k - 1], device_at(peer, core)))

    def stage3(p):
        lo, width, order = PARTS[p]
        held, got = buffers[6 * p + 4 : 6 * p + 6]
        for copy in sent[p][-3:]:
            copy.wait_recv()
        return held[spot[order[2]]] + got[0] + got[1] + got[2]

    backward(BANDS - 1)
    for p in range(3):
        stage0(p)
    for a in range(BANDS - 1):
        backward(a)
    for p in range(3):
        stage1(p)

    me = lat * lons + lon
    picked = lax.broadcasted_iota(jnp.int32, (8, C), 0) + me * 4
    picked = (picked == lax.broadcasted_iota(jnp.int32, (8, C), 1)).astype(F32)
    w_rows = nn(picked.astype(BF16), wqkv[...])
    gain_rows = jnp.sum(picked * gain[...], axis=1, keepdims=True)

    for copy in back:
        copy.wait_recv()
    for a in range(BANDS):
        edge = nn(spread[...], left[a * SIDE : (a + 1) * SIDE])
        rows = BAND if a < BANDS - 1 else BAND - LEAD
        start = a * BAND
        out_ref[LEAD + start : LEAD + start + rows] = (
            out_ext[start : start + rows].astype(F32) + edge[:rows]
        ).astype(BF16)
    edge = nn(spread[...], back_corner[...])
    out_ref[0:LEAD] = (top[...].astype(F32) + edge[BAND - LEAD :]).astype(BF16)

    for p in range(3):
        stage2(p)
    total = jnp.concatenate([stage3(p) for p in range(3)], axis=1)
    total = total * (1.0 / math.sqrt(TOKENS * lats * lons))
    gqkv = [total[4 * j : 4 * j + 4] for j in range(3)]
    gqkv_ref[...] = jnp.concatenate(gqkv, axis=1)
    gproj_ref[...] = total[12:16]
    dots = jnp.zeros((4, 1), F32)
    for j in range(3):
        dots = dots + jnp.sum(gqkv[j] * w_rows[0:4, j * C : (j + 1) * C], axis=1, keepdims=True)
    dots = dots / gain_rows[0:4]
    ggain_ref[...] = jnp.broadcast_to(dots, (4, 128))
    for copy in halo + first + back + [c for part in sent for c in part]:
        copy.wait_send()


def sublayer(*args):
    vmem = pl.BlockSpec(memory_space=pltpu.VMEM)
    hbm = pl.BlockSpec(memory_space=pl.ANY)
    scratch = [
        pltpu.VMEM((2, TOKENS + LEAD, C), BF16),
        pltpu.VMEM((2, BANDS * SIDE, C), BF16),
        pltpu.VMEM((2, BANDS * SIDE, C), BF16),
        pltpu.VMEM((2, SIDE, C), BF16),
        pltpu.VMEM((2, SIDE, C), BF16),
        pltpu.VMEM((C, 3 * C), BF16),
        pltpu.VMEM((C, C), BF16),
        pltpu.VMEM((TOKENS, C), F32),
        pltpu.VMEM((TOKENS, 128), F32),
        pltpu.VMEM((TOKENS, C), BF16),
        pltpu.VMEM((TOKENS, C), BF16),
        pltpu.VMEM((C, TOKENS), BF16),
        pltpu.VMEM((C, TOKENS), BF16),
        pltpu.VMEM((TOKENS, 3 * C), F32),
        pltpu.VMEM((TOKENS, C), F32),
        pltpu.VMEM((TOKENS, C), F32),
        pltpu.VMEM((TOKENS, 3 * C), F32),
        pltpu.VMEM((TOKENS, C), BF16),
        pltpu.VMEM((BANDS * SIDE, C), BF16),
        pltpu.VMEM((LEAD, C), BF16),
        pltpu.VMEM((BANDS * SIDE, C), BF16),
        pltpu.VMEM((SIDE, C), BF16),
        pltpu.VMEM((4, C, 256), F32),
        pltpu.VMEM((64, 16, C), F32),
        pltpu.VMEM((64, 16, C), BF16),
        pltpu.VMEM((64, 16, C), BF16),
    ]
    for _, width, _ in PARTS:
        for i, dims in enumerate(((4, 4, 4), (3, 4, 4), (4, 4), (3, 4), (4,), (3,))):
            scratch.append(pltpu.VMEM(dims + (16, width), BF16 if i < 2 else F32))
    copies = 3 + 6 + 10 * len(PARTS)
    return pl.pallas_call(
        sublayer_kernel,
        out_shape=(
            jax.ShapeDtypeStruct((TOKENS, C), BF16),
            jax.ShapeDtypeStruct((4, 3 * C), F32),
            jax.ShapeDtypeStruct((4, C), F32),
            jax.ShapeDtypeStruct((4, 128), F32),
        ),
        in_specs=[hbm, hbm, vmem, hbm, hbm, vmem, vmem, vmem],
        out_specs=(vmem,) * 4,
        scratch_shapes=scratch
        + [
            pltpu.SemaphoreType.DMA((4,)),
            pltpu.SemaphoreType.DMA((copies,)),
            pltpu.SemaphoreType.DMA((copies,)),
        ],
        compiler_params=pltpu.CompilerParams(
            collective_id=1, has_side_effects=True, vmem_limit_bytes=62 * 1024 * 1024
        ),
        name="window_grads",
    )(*args)


def on_device(activations, cotangent, norm_gain, qkv_weight, proj_weight):
    perm = window_order()
    spread = np.zeros((BAND, SIDE), np.float32)
    for r in range(WIN_LAT):
        for c in range(HALF_LON):
            spread[r * COLS + c, r * HALF_LON + c] = 1.0
    grad_input, gqkv, gproj, ggain = sublayer(
        activations.reshape(TOKENS, C),
        cotangent.reshape(TOKENS, C),
        norm_gain.reshape(1, C),
        qkv_weight,
        proj_weight,
        jnp.asarray(perm, BF16),
        jnp.asarray(perm.T, BF16),
        jnp.asarray(spread, BF16),
    )
    return grad_input.reshape(ROWS, COLS, C), gqkv, gproj, ggain[:, 0]


def solution(mesh):
    return jax.shard_map(
        on_device,
        mesh=mesh,
        in_specs=(P("lat", "lon", None), P("lat", "lon", None), P(), P(), P()),
        out_specs=(
            P("lat", "lon", None),
            P(("lat", "lon"), None),
            P(("lat", "lon"), None),
            P(("lat", "lon")),
        ),
        check_vma=False,
    )
```

time: 241 us -> 73.9 us (0.31)
  waiting for transfers between devices: 163 us -> 0 us
  Pallas kernels: 41.7 us -> 68.2 us
  between operations: 14.2 us -> 0.64 us
  starting transfers between devices: 9.12 us -> 0 us
  other arithmetic: 7.52 us -> 0 us
    unnamed x2 -> x0, waiting for transfers between devices: 137 us -> none
    pallas_call x1, Pallas kernels: 41.7 us -> 68.2 us  [sublayer(): pl.pallas_call(sublayer_kernel, out_shape=(jax.ShapeDtypeStruct((TOKENS,...]
    ppermute x4 -> x0, waiting for transfers between devices: 26 us -> none  [shifted(): lax.ppermute(shard, axis, [(i, (i + by) % peers) for i in range(peers)])]
    ppermute x4 -> x0, starting transfers between devices: 9.08 us -> none  [shifted(): lax.ppermute(shard, axis, [(i, (i + by) % peers) for i in range(peers)])]
  transfers between devices with their start and end apart: 5 -> 0, of which waited for: 5 -> 0; matrix products, arithmetic and copies ran while one was open for 1% -> 0% of each run, Pallas kernels for 0% -> 0%
where the time goes in v2:
time: 73.9 us; the launch traced here: 73.7 us
  Pallas kernels  68.2 us (92%)
  local copies, waits for them, and re-layouts  4.9 us (7%)
    pallas_call x1, Pallas kernels, sublayer(): pl.pallas_call(sublayer_kernel, out_shape=(jax.ShapeDtypeStruct((TOKENS,...  68.2 us
    unnamed x7, local copies, waits for them, and re-layouts  3.59 us

profile of v2, /device:TPU:0, one launch (start us, length us, event | category | flops | bytes accessed | tf_op | source)
XLA Modules:
  0.0 73.7 jit_solution(9314782187336616280)
XLA Ops:
  0.6 68.2 %window_grads.1 = (bf16[1152,512]{1,0:T(8,128)(2,1)}, f32[4,1536]{1,0:T(4,128)}, f32[4,512]{1,0:T(4,128)}, f32[4,128]{1,0:T(4,128)}) custom-call(bf16[1152,512]{1,0:T(8,128)(2,1)} %bitcast.5, bf16[1152,512]{1,0:T(8,128)(2,1)} %bitcast.6, f32[1,512]{1,0:T(1,128)} %bitcast.7, bf16[512,1536]{1,0:T(8,128)(2,1)} %wqkv_hbm.1, bf16[512,512]{1,0:T(8,128)(2,1)} %wproj_hbm.1, ...), custom_call_target="tpu_custom_call" | custom-call | tf_op jit(solution)/shard_map/window_grads/pallas_call | solution.py:425
  68.8 1.3 %slice_reduce_fusion = f32[4]{0:T(128)} fusion(f32[4,128]{1,0:T(4,128)} %get-tuple-element.11), kind=kLoop, calls=%fused_computation | loop fusion | bytes 32 | tf_op jit(solution)/shard_map/slice | solution.py:464
  70.1 0.0 copy-start
  70.1 0.0 copy-start.1
  70.1 2.4 %copy.15 = bf16[24,48,512]{2,1,0:T(8,128)(2,1)} copy(bf16[24,48,512]{2,1,0:T(8,128)(2,1)} %bitcast.4) | data formatting | bytes 2359296
  72.5 0.0 copy-done
  72.5 0.6 copy.16
  73.1 0.0 copy-done.1
  73.1 0.6 copy.17
Async XLA Ops:
  70.1 2.4 %copy-start = (f32[4,1536]{1,0:T(4,128)S(1)}, f32[4,1536]{1,0:T(4,128)}, u32[]{:S(2)}) copy-start(f32[4,1536]{1,0:T(4,128)} %get-tuple-element.17) | copy-start | bytes 73732
  70.1 3.0 %copy-start.1 = (f32[4,512]{1,0:T(4,128)S(1)}, f32[4,512]{1,0:T(4,128)}, u32[]{:S(2)}) copy-start(f32[4,512]{1,0:T(4,128)} %get-tuple-element.18) | copy-start | bytes 24580

commit v3 on v2

--- a/solution.py
+++ b/solution.py
@@ -172,6 +172,7 @@
     key_half = lax.broadcasted_iota(jnp.int32, (SPAN, SPAN), 0) >= HALF_LAT * WIN_LON
     query_half = lax.broadcasted_iota(jnp.int32, (SPAN, SPAN), 1) >= HALF_LAT * WIN_LON
     parted = jnp.where(key_half == query_half, 0.0, -1e30)
+    parted = jnp.concatenate([parted] * GROUP, axis=1)
 
     def stacked(x):
         return jnp.concatenate([x * m for m in masks], axis=0).astype(BF16)
@@ -185,47 +186,55 @@
 
     scale = HEAD ** (-0.5)
 
-    def attention(w):
-        rows = pl.ds(pl.multiple_of(w * SPAN, 8), SPAN)
-        edge = jnp.where((lat == lats - 1) & (w >= (BANDS - 1) * PER_BAND), 1.0, 0.0)
+    def attention(pair):
+        edge = jnp.where((lat == lats - 1) & (pair >= (BANDS - 1) * PER_BAND // 2), 1.0, 0.0)
         shut = parted * edge
-        for g in range(C // 128):
-            cols = slice(g * 128, (g + 1) * 128)
-            q = qkv[rows, g * 128 : (g + 1) * 128].astype(BF16)
-            k_st = stacked(qkv[rows, C + g * 128 : C + (g + 1) * 128])
-            v_st = stacked(qkv[rows, 2 * C + g * 128 : 2 * C + (g + 1) * 128])
-            da = grad_att[rows, cols].astype(BF16)
-            s = nt(k_st, q).reshape(GROUP, SPAN, SPAN) * scale + shut
-            ex = jnp.exp(s - jnp.max(s, axis=1, keepdims=True))
-            prob = ex * (1.0 / jnp.sum(ex, axis=1, keepdims=True))
-            gp = nt(v_st, da).reshape(GROUP, SPAN, SPAN)
-            inner = jnp.sum(prob * gp, axis=1, keepdims=True)
-            gs = (prob * (gp - inner) * scale).reshape(GROUP * SPAN, SPAN).astype(BF16)
-            pb = prob.reshape(GROUP * SPAN, SPAN).astype(BF16)
-            att[rows, cols] = tn(pb, v_st)
-            grad_all[rows, g * 128 : (g + 1) * 128] = tn(gs, k_st)
-            grad_all[rows, C + g * 128 : C + (g + 1) * 128] = by_head(nn(gs, q))
-            grad_all[rows, 2 * C + g * 128 : 2 * C + (g + 1) * 128] = by_head(nn(pb, da))
+        todo = []
+        for i in range(2):
+            rows = pl.ds(pl.multiple_of(pair * PAIR + i * SPAN, 8), SPAN)
+            todo += [(rows, [slice(j * C + lo, j * C + lo + 128) for j in range(3)])
+                     for lo in range(0, C, 128)]
+        q = [stacked(qkv[rows, cols[0]]) for rows, cols in todo]
+        k = [qkv[rows, cols[1]].astype(BF16) for rows, cols in todo]
+        v = [qkv[rows, cols[2]].astype(BF16) for rows, cols in todo]
+        da = [stacked(grad_att[rows, cols[0]]) for rows, cols in todo]
+        n = range(len(todo))
+        s = [nt(k[i], q[i]) * scale + shut for i in n]
+        gp = [nt(v[i], da[i]) for i in n]
+        ex = [jnp.exp(x - jnp.max(x, axis=0, keepdims=True)) for x in s]
+        prob = [x * (1.0 / jnp.sum(x, axis=0, keepdims=True)) for x in ex]
+        inner = [jnp.sum(prob[i] * gp[i], axis=0, keepdims=True) for i in n]
+        gs = [(prob[i] * (gp[i] - inner[i]) * scale).astype(BF16) for i in n]
+        pb = [x.astype(BF16) for x in prob]
+        found = [by_head(tn(pb[i], v[i])) for i in n]
+        grad_q = [by_head(tn(gs[i], k[i])) for i in n]
+        grad_k = [nn(gs[i], q[i]) for i in n]
+        grad_v = [nn(pb[i], da[i]) for i in n]
+        for i, (rows, cols) in enumerate(todo):
+            att[rows, cols[0]] = found[i]
+            grad_all[rows, cols[0]] = grad_q[i]
+            grad_all[rows, cols[1]] = grad_k[i]
+            grad_all[rows, cols[2]] = grad_v[i]
 
     loads[2].wait()
     loads[3].wait()
     forward([(a, 0) for a in range(BANDS - 1)])
 
     def early(i, carry):
-        attention(i // 2 * PER_BAND + i % 2)
+        attention(i * 2)
         return carry
 
-    lax.fori_loop(0, 2 * (BANDS - 1), early, 0)
+    lax.fori_loop(0, BANDS - 1, early, 0)
     for copy in halo:
         copy.wait_recv()
     forward([(a, 1) for a in range(BANDS - 1)])
     forward([(BANDS - 1, 0), (BANDS - 1, 1)])
 
     def late(i, carry):
-        attention(jnp.where(i < 6, i // 2 * PER_BAND + 2 + i % 2, i + 6))
+        attention(jnp.where(i < BANDS - 1, i * 2 + 1, i + BANDS - 1))
         return carry
 
-    lax.fori_loop(0, 2 * (BANDS + 1), late, 0)
+    lax.fori_loop(0, BANDS + 1, late, 0)
 
     scaled_t[...] = scaled[...].T
     att_t[...] = att[...].astype(BF16).T

time: 73.9 us -> 65.3 us (0.88)
  Pallas kernels: 68.2 us -> 59.6 us
    pallas_call x1, Pallas kernels: 68.2 us -> 59.6 us  [sublayer(): pl.pallas_call(sublayer_kernel, out_shape=(jax.ShapeDtypeStruct((TOKENS,...]
where the time goes in v3:
time: 65.3 us; the launch traced here: 65.1 us
  Pallas kernels  59.6 us (91%)
  local copies, waits for them, and re-layouts  4.9 us (8%)
    pallas_call x1, Pallas kernels, sublayer(): pl.pallas_call(sublayer_kernel, out_shape=(jax.ShapeDtypeStruct((TOKENS,...  59.6 us
    unnamed x7, local copies, waits for them, and re-layouts  3.59 us
    slice x1, local copies, waits for them, and re-layouts, on_device(): return (grad_input.reshape(ROWS, COLS, C), gqkv, gproj, ggain[:, 0])  1.31 us

profile of v3, /device:TPU:0, one launch (start us, length us, event | category | flops | bytes accessed | tf_op | source)
XLA Modules:
  0.0 65.1 jit_solution(17563117968079992958)
XLA Ops:
  0.6 59.6 %window_grads.1 = (bf16[1152,512]{1,0:T(8,128)(2,1)}, f32[4,1536]{1,0:T(4,128)}, f32[4,512]{1,0:T(4,128)}, f32[4,128]{1,0:T(4,128)}) custom-call(bf16[1152,512]{1,0:T(8,128)(2,1)} %bitcast.5, bf16[1152,512]{1,0:T(8,128)(2,1)} %bitcast.6, f32[1,512]{1,0:T(1,128)} %bitcast.7, bf16[512,1536]{1,0:T(8,128)(2,1)} %wqkv_hbm.1, bf16[512,512]{1,0:T(8,128)(2,1)} %wproj_hbm.1, ...), custom_call_target="tpu_custom_call" | custom-call | tf_op jit(solution)/shard_map/window_grads/pallas_call | solution.py:434
  60.2 1.3 %slice_reduce_fusion = f32[4]{0:T(128)} fusion(f32[4,128]{1,0:T(4,128)} %get-tuple-element.11), kind=kLoop, calls=%fused_computation | loop fusion | bytes 32 | tf_op jit(solution)/shard_map/slice | solution.py:473
  61.5 0.0 copy-start
  61.5 0.0 copy-start.1
  61.5 2.4 %copy.15 = bf16[24,48,512]{2,1,0:T(8,128)(2,1)} copy(bf16[24,48,512]{2,1,0:T(8,128)(2,1)} %bitcast.4) | data formatting | bytes 2359296
  63.9 0.0 copy-done
  63.9 0.6 copy.16
  64.5 0.0 copy-done.1
  64.5 0.6 copy.17
Async XLA Ops:
  61.5 2.4 %copy-start = (f32[4,1536]{1,0:T(4,128)S(1)}, f32[4,1536]{1,0:T(4,128)}, u32[]{:S(2)}) copy-start(f32[4,1536]{1,0:T(4,128)} %get-tuple-element.17) | copy-start | bytes 73732
  61.5 3.0 %copy-start.1 = (f32[4,512]{1,0:T(4,128)S(1)}, f32[4,512]{1,0:T(4,128)}, u32[]{:S(2)}) copy-start(f32[4,512]{1,0:T(4,128)} %get-tuple-element.18) | copy-start | bytes 24580

commit v4 on v3

--- a/solution.py
+++ b/solution.py
@@ -51,10 +51,9 @@
     return lax.dot_general(a, b, (((0,), (0,)), ((), ())), preferred_element_type=F32)
 
 
-PARTS = ((0, 256, "zyx"), (256, 128, "xzy"), (384, 128, "yxz"))
+PARTS = ((0, 256, "zyx", "xzy"), (256, 128, "xzy", "yxz"), (384, 128, "yxz", "zyx"))
 MESH = pl.DeviceIdType.MESH
 LEAD = HALF_LAT * COLS
-PAIR = 2 * SPAN
 
 
 def place():
@@ -67,21 +66,17 @@
     return (spot["z"] * 2 + spot["x"] % 2, spot["y"] * 4 + spot["x"] // 2 * 2 + core)
 
 
-def along(spot, axis, by):
-    return {**spot, axis: (spot[axis] + by) % 4}
-
-
 def chip_at(at):
     return at["z"] * 16 + at["x"] % 2 * 8 + at["y"] * 2 + at["x"] // 2
 
 
 def sublayer_kernel(
     own_in, own_cot, gain, wqkv_hbm, wproj_hbm, perm, perm_t, spread,
-    out_ref, gqkv_ref, gproj_ref, ggain_ref,
+    out_hbm, gqkv_ref, gproj_ref, ggain_ref,
     ext, side, side_out, corner, corner_out, wqkv, wproj,
     normed, inv_std, scaled, cot_win, scaled_t, att_t, qkv, grad_att, att, grad_all,
     out_ext, back_side, top, left, back_corner, grads, mine, theirs, got0,
-    *rest,
+    out_ref, *rest,
 ):
     buffers, (local, send, recv) = rest[:-3], rest[-3:]
     loads = [
@@ -99,8 +94,13 @@
     down, up = (lat + 1) % lats, (lat + lats - 1) % lats
     east, west = (lon + 1) % lons, (lon + lons - 1) % lons
     peers = [sibling, (down, lon), (up, lon), (lat, east), (lat, west), (down, east), (up, west)]
-    for axis in "xyz":
-        peers += [device_at(along(spot, axis, k), core) for k in (1, 2, 3)]
+    for i in range(4):
+        for j in range(4):
+            for axes in ("xy", "yz", "zx") if i and j else ("x", "y", "z") if i else ():
+                if j == 0 or len(axes) == 2:
+                    steps = dict(zip(axes, (i, j)))
+                    there = {axis: (spot[axis] + steps.get(axis, 0)) % 4 for axis in "xyz"}
+                    peers.append(device_at(there, core))
     barrier = pltpu.get_barrier_semaphore()
     for peer in peers:
         pl.semaphore_signal(barrier, inc=1, device_id=peer, device_id_type=MESH)
@@ -138,30 +138,34 @@
         gathered = []
         for i in range(2):
             parts = []
-            for a, half in pieces:
+            for a, lo, hi in pieces:
                 start = LEAD + a * BAND
                 src = ext[i, start : start + BAND]
-                rows = perm[half * PAIR : (half + 1) * PAIR]
-                if half == 0:
-                    parts.append(nn(rows[:, :BAND], src))
+                first_row, last_row = lo // 16 * 16, -(-hi // 16) * 16
+                rows = perm[first_row:last_row]
+                if hi < BAND:
+                    got = nn(rows[:, :BAND], src)
                 else:
                     edge = side[i, a * SIDE : (a + 1) * SIDE]
                     if a == BANDS - 1:
                         edge = (edge.astype(F32) + corner[i].astype(F32)).astype(BF16)
-                    parts.append(nn(rows, jnp.concatenate([src, edge], axis=0)))
+                    got = nn(rows, jnp.concatenate([src, edge], axis=0))
+                parts.append(got[lo - first_row : hi - first_row])
             gathered.append(jnp.concatenate(parts, axis=0))
-        x, cot = gathered[0], gathered[1].astype(BF16)
+        x, cot = gathered
         center = x - jnp.mean(x, axis=-1, keepdims=True)
         inv = lax.rsqrt(jnp.mean(center * center, axis=-1, keepdims=True) + 1e-05)
         norm = center * inv
-        sc = (norm * gain[...]).astype(BF16)
-        qkv_now = nn(sc, wqkv[...]).astype(BF16).astype(F32)
-        att_now = nt(cot, wproj[...]).astype(BF16).astype(F32)
-        for i, (a, half) in enumerate(pieces):
-            dst = slice(a * BAND + half * PAIR, a * BAND + (half + 1) * PAIR)
-            src = slice(i * PAIR, (i + 1) * PAIR)
+        sc = norm * gain[...]
+        qkv_now = nn(sc.astype(BF16), wqkv[...]).astype(BF16).astype(F32)
+        att_now = nt(cot.astype(BF16), wproj[...]).astype(BF16).astype(F32)
+        at = 0
+        for a, lo, hi in pieces:
+            dst = slice(a * BAND + lo, a * BAND + hi)
+            src = slice(at, at + hi - lo)
+            at += hi - lo
             normed[dst] = norm[src]
-            inv_std[dst] = jnp.broadcast_to(inv[src], (PAIR, 128))
+            inv_std[dst] = jnp.broadcast_to(inv[src], (hi - lo, 128))
             scaled[dst] = sc[src]
             cot_win[dst] = cot[src]
             qkv[dst] = qkv_now[src]
@@ -186,12 +190,11 @@
 
     scale = HEAD ** (-0.5)
 
-    def attention(pair):
-        edge = jnp.where((lat == lats - 1) & (pair >= (BANDS - 1) * PER_BAND // 2), 1.0, 0.0)
-        shut = parted * edge
+    def attention(windows, edge=False):
+        shut = parted * jnp.where(lat == lats - 1, 1.0, 0.0)
         todo = []
-        for i in range(2):
-            rows = pl.ds(pl.multiple_of(pair * PAIR + i * SPAN, 8), SPAN)
+        for w in windows:
+            rows = pl.ds(pl.multiple_of(w * SPAN, 8), SPAN)
             todo += [(rows, [slice(j * C + lo, j * C + lo + 128) for j in range(3)])
                      for lo in range(0, C, 128)]
         q = [stacked(qkv[rows, cols[0]]) for rows, cols in todo]
@@ -199,7 +202,9 @@
         v = [qkv[rows, cols[2]].astype(BF16) for rows, cols in todo]
         da = [stacked(grad_att[rows, cols[0]]) for rows, cols in todo]
         n = range(len(todo))
-        s = [nt(k[i], q[i]) * scale + shut for i in n]
+        s = [nt(k[i], q[i]) * scale for i in n]
+        if edge:
+            s = [x + shut for x in s]
         gp = [nt(v[i], da[i]) for i in n]
         ex = [jnp.exp(x - jnp.max(x, axis=0, keepdims=True)) for x in s]
         prob = [x * (1.0 / jnp.sum(x, axis=0, keepdims=True)) for x in ex]
@@ -218,25 +223,27 @@
 
     loads[2].wait()
     loads[3].wait()
-    forward([(a, 0) for a in range(BANDS - 1)])
+    inner = (PER_BAND - 1) * SPAN
+    forward([(a, 0, inner) for a in range(BANDS - 1)])
 
     def early(i, carry):
-        attention(i * 2)
+        attention([i * PER_BAND + b for b in range(PER_BAND - 1)])
         return carry
 
     lax.fori_loop(0, BANDS - 1, early, 0)
     for copy in halo:
         copy.wait_recv()
-    forward([(a, 1) for a in range(BANDS - 1)])
-    forward([(BANDS - 1, 0), (BANDS - 1, 1)])
+    forward([(a, inner, BAND) for a in range(BANDS - 1)])
+    forward([(BANDS - 1, 0, BAND)])
+    attention([a * PER_BAND + PER_BAND - 1 for a in range(BANDS - 1)])
 
     def late(i, carry):
-        attention(jnp.where(i < BANDS - 1, i * 2 + 1, i + BANDS - 1))
+        attention([(BANDS - 1) * PER_BAND + 2 * i + b for b in range(2)], edge=True)
         return carry
 
-    lax.fori_loop(0, BANDS + 1, late, 0)
-
-    scaled_t[...] = scaled[...].T
+    lax.fori_loop(0, PER_BAND // 2, late, 0)
+
+    scaled_t[...] = scaled[...].astype(BF16).T
     att_t[...] = att[...].astype(BF16).T
     upper = lax.broadcasted_iota(jnp.int32, (1, 8, 1), 1) < 4
     first_core = lax.broadcasted_iota(jnp.int32, (1, 8, 1), 1) * 0 + core == 0
@@ -247,7 +254,7 @@
         for j in range(3):
             cols = slice(j * C + lo, j * C + lo + 256)
             grads[j] = nn(scaled_t[...], grad_all[:, cols].astype(BF16))
-        grads[3] = nn(att_t[...], cot_win[:, lanes])
+        grads[3] = nn(att_t[...], cot_win[:, lanes].astype(BF16))
 
         def pack(i, carry):
             rows = pl.ds(pl.multiple_of(i * 64, 64), 64)
@@ -267,7 +274,7 @@
             return carry
 
         lax.fori_loop(0, 8, pack, 0)
-        for start, width, _ in PARTS:
+        for start, width, _, _ in PARTS:
             if lo <= start < lo + 256:
                 span = pl.ds(start, width)
                 first.append(remote(theirs.at[:, :, span], got0.at[:, :, span], sibling))
@@ -283,7 +290,7 @@
             - jnp.mean(gn, axis=-1, keepdims=True)
             - norm * jnp.mean(gn * norm, axis=-1, keepdims=True)
         )
-        done = (cot_win[dst].astype(F32) + branch).astype(BF16)
+        done = (cot_win[dst] + branch).astype(BF16)
         slab = nn(perm_t[...], done).astype(BF16)
         out_ext[dst] = slab[:BAND]
         edge = slice(a * SIDE, (a + 1) * SIDE)
@@ -294,69 +301,85 @@
             back.append(remote(back_side.at[edge], back_corner, (down, east)))
         back.append(remote(back_side.at[edge], left.at[edge], (lat, east)))
 
+    def role(p, r, axis):
+        first_order, second_order = PARTS[p][2:]
+        return (1 - core) * int(first_order[r] == axis) + core * int(second_order[r] == axis)
+
+    def by_role(p, steps):
+        return {axis: sum(role(p, r, axis) * steps[r] for r in range(3)) for axis in "xyz"}
+
+    def my_role(p, r):
+        return sum(role(p, r, axis) * spot[axis] for axis in "xyz")
+
+    def peer_at(p, steps):
+        moved = by_role(p, steps)
+        return device_at({axis: (spot[axis] + moved[axis]) % 4 for axis in "xyz"}, core)
+
     def summed0(p, chip):
-        lo, width, _ = PARTS[p]
+        lo, width = PARTS[p][:2]
         lanes = slice(lo, lo + width)
         return mine[chip, :, lanes] + got0[chip, :, lanes].astype(F32)
 
     sent = [[] for _ in PARTS]
 
     def stage0(p):
-        lo, width, order = PARTS[p]
-        held = buffers[6 * p]
+        held, got = buffers[5 * p : 5 * p + 2]
         first[p].wait_recv()
 
         def add(i, carry):
-            at = dict(zip(order, (i // 16, i // 4 % 4, i % 4)))
-            held[i // 16, i // 4 % 4, i % 4] = summed0(p, chip_at(at)).astype(BF16)
+            at = (i // 16, i // 4 % 4, i % 4)
+            held[at] = summed0(p, chip_at(by_role(p, at))).astype(BF16)
             return carry
 
         lax.fori_loop(0, 64, add, 0)
-        for k in (1, 2, 3):
-            peer = along(spot, order[0], k)
+        for k in (2, 1, 3):
             sent[p].append(
-                remote(held.at[peer[order[0]]], buffers[6 * p + 1].at[k - 1], device_at(peer, core))
+                remote(held.at[(my_role(p, 0) + k) % 4], got.at[k - 1], peer_at(p, (k, 0, 0)))
             )
 
     def stage1(p):
-        lo, width, order = PARTS[p]
-        got, nxt, nxt_got = buffers[6 * p + 1 : 6 * p + 4]
-        for copy in sent[p][-3:]:
+        got, nxt, nxt_got, keep = buffers[5 * p + 1 : 5 * p + 5]
+        for copy in sent[p]:
             copy.wait_recv()
+        here = my_role(p, 0)
+        b, c = my_role(p, 1), my_role(p, 2)
+
+        def total(i, j):
+            x = summed0(p, chip_at(by_role(p, (here, i, j))))
+            for k in range(3):
+                x = x + got[k, i, j].astype(F32)
+            return x
 
         def add(i, carry):
-            at = dict(zip(order, (spot[order[0]], i // 4, i % 4)))
-            total = summed0(p, chip_at(at))
-            for k in range(3):
-                total = total + got[k, i // 4, i % 4].astype(F32)
-            nxt[i // 4, i % 4] = total
+            nxt[i // 4, i % 4] = total(i // 4, i % 4).astype(BF16)
             return carry
 
         lax.fori_loop(0, 16, add, 0)
-        for k in (1, 2, 3):
-            peer = along(spot, order[1], k)
-            sent[p].append(remote(nxt.at[peer[order[1]]], nxt_got.at[k - 1], device_at(peer, core)))
+        keep[...] = total(b, c)
+        for i in (2, 1, 3, 0):
+            for j in (2, 1, 3, 0):
+                if i or j:
+                    sent[p].append(
+                        remote(
+                            nxt.at[(b + i) % 4, (c + j) % 4],
+                            nxt_got.at[4 * i + j - 1],
+                            peer_at(p, (0, i, j)),
+                        )
+                    )
 
     def stage2(p):
-        lo, width, order = PARTS[p]
-        held, got, nxt, nxt_got = buffers[6 * p + 2 : 6 * p + 6]
-        for copy in sent[p][-3:]:
+        got, keep = buffers[5 * p + 3 : 5 * p + 5]
+        for copy in sent[p][3:]:
             copy.wait_recv()
-        nxt[...] = held[spot[order[1]]] + got[0] + got[1] + got[2]
-        for k in (1, 2, 3):
-            peer = along(spot, order[2], k)
-            sent[p].append(remote(nxt.at[peer[order[2]]], nxt_got.at[k - 1], device_at(peer, core)))
-
-    def stage3(p):
-        lo, width, order = PARTS[p]
-        held, got = buffers[6 * p + 4 : 6 * p + 6]
-        for copy in sent[p][-3:]:
-            copy.wait_recv()
-        return held[spot[order[2]]] + got[0] + got[1] + got[2]
-
+        x = keep[...]
+        for i in range(15):
+            x = x + got[i].astype(F32)
+        return x
+
+    stage0(0)
     backward(BANDS - 1)
-    for p in range(3):
-        stage0(p)
+    stage0(1)
+    stage0(2)
     for a in range(BANDS - 1):
         backward(a)
     for p in range(3):
@@ -379,10 +402,10 @@
         ).astype(BF16)
     edge = nn(spread[...], back_corner[...])
     out_ref[0:LEAD] = (top[...].astype(F32) + edge[BAND - LEAD :]).astype(BF16)
-
-    for p in range(3):
-        stage2(p)
-    total = jnp.concatenate([stage3(p) for p in range(3)], axis=1)
+    store = pltpu.make_async_copy(out_ref, out_hbm, local.at[4])
+    store.start()
+
+    total = jnp.concatenate([stage2(p) for p in range(3)], axis=1)
     total = total * (1.0 / math.sqrt(TOKENS * lats * lons))
     gqkv = [total[4 * j : 4 * j + 4] for j in range(3)]
     gqkv_ref[...] = jnp.concatenate(gqkv, axis=1)
@@ -391,9 +414,12 @@
     for j in range(3):
         dots = dots + jnp.sum(gqkv[j] * w_rows[0:4, j * C : (j + 1) * C], axis=1, keepdims=True)
     dots = dots / gain_rows[0:4]
-    ggain_ref[...] = jnp.broadcast_to(dots, (4, 128))
+    diagonal = lax.broadcasted_iota(jnp.int32, (4, 128), 0)
+    diagonal = diagonal == lax.broadcasted_iota(jnp.int32, (4, 128), 1)
+    ggain_ref[...] = jnp.sum(jnp.where(diagonal, dots, 0.0), axis=0, keepdims=True)
     for copy in halo + first + back + [c for part in sent for c in part]:
         copy.wait_send()
+    store.wait()
 
 
 def sublayer(*args):
@@ -409,8 +435,8 @@
         pltpu.VMEM((C, C), BF16),
         pltpu.VMEM((TOKENS, C), F32),
         pltpu.VMEM((TOKENS, 128), F32),
-        pltpu.VMEM((TOKENS, C), BF16),
-        pltpu.VMEM((TOKENS, C), BF16),
+        pltpu.VMEM((TOKENS, C), F32),
+        pltpu.VMEM((TOKENS, C), F32),
         pltpu.VMEM((C, TOKENS), BF16),
         pltpu.VMEM((C, TOKENS), BF16),
         pltpu.VMEM((TOKENS, 3 * C), F32),
@@ -426,24 +452,26 @@
         pltpu.VMEM((64, 16, C), F32),
         pltpu.VMEM((64, 16, C), BF16),
         pltpu.VMEM((64, 16, C), BF16),
+        pltpu.VMEM((TOKENS, C), BF16),
     ]
-    for _, width, _ in PARTS:
-        for i, dims in enumerate(((4, 4, 4), (3, 4, 4), (4, 4), (3, 4), (4,), (3,))):
-            scratch.append(pltpu.VMEM(dims + (16, width), BF16 if i < 2 else F32))
-    copies = 3 + 6 + 10 * len(PARTS)
+    for _, width, _, _ in PARTS:
+        for dims in ((4, 4, 4), (3, 4, 4), (4, 4), (15,)):
+            scratch.append(pltpu.VMEM(dims + (16, width), BF16))
+        scratch.append(pltpu.VMEM((16, width), F32))
+    copies = 3 + 6 + 19 * len(PARTS)
     return pl.pallas_call(
         sublayer_kernel,
         out_shape=(
             jax.ShapeDtypeStruct((TOKENS, C), BF16),
             jax.ShapeDtypeStruct((4, 3 * C), F32),
             jax.ShapeDtypeStruct((4, C), F32),
-            jax.ShapeDtypeStruct((4, 128), F32),
+            jax.ShapeDtypeStruct((1, 128), F32),
         ),
         in_specs=[hbm, hbm, vmem, hbm, hbm, vmem, vmem, vmem],
-        out_specs=(vmem,) * 4,
+        out_specs=(hbm, vmem, vmem, vmem),
         scratch_shapes=scratch
         + [
-            pltpu.SemaphoreType.DMA((4,)),
+            pltpu.SemaphoreType.DMA((5,)),
             pltpu.SemaphoreType.DMA((copies,)),
             pltpu.SemaphoreType.DMA((copies,)),
         ],
@@ -454,13 +482,39 @@
     )(*args)
 
 
+def hand_on_kernel(out_ref, gqkv_ref, gproj_ref, gain_ref, out, gqkv, gproj, ggain, sem):
+    copy = pltpu.make_async_copy(out_ref, out, sem)
+    copy.start()
+    gqkv[...] = gqkv_ref[...]
+    gproj[...] = gproj_ref[...]
+    ggain[...] = gain_ref[0, 0:4]
+    copy.wait()
+
+
+def hand_on(*args):
+    vmem = pl.BlockSpec(memory_space=pltpu.VMEM)
+    return pl.pallas_call(
+        hand_on_kernel,
+        out_shape=(
+            jax.ShapeDtypeStruct((TOKENS, C), BF16),
+            jax.ShapeDtypeStruct((4, 3 * C), F32),
+            jax.ShapeDtypeStruct((4, C), F32),
+            jax.ShapeDtypeStruct((4,), F32),
+        ),
+        in_specs=[vmem] * 4,
+        out_specs=(pl.BlockSpec(memory_space=pl.ANY), vmem, vmem, vmem),
+        scratch_shapes=[pltpu.SemaphoreType.DMA],
+        name="hand_on",
+    )(*args)
+
+
 def on_device(activations, cotangent, norm_gain, qkv_weight, proj_weight):
     perm = window_order()
     spread = np.zeros((BAND, SIDE), np.float32)
     for r in range(WIN_LAT):
         for c in range(HALF_LON):
             spread[r * COLS + c, r * HALF_LON + c] = 1.0
-    grad_input, gqkv, gproj, ggain = sublayer(
+    results = sublayer(
         activations.reshape(TOKENS, C),
         cotangent.reshape(TOKENS, C),
         norm_gain.reshape(1, C),
@@ -470,7 +524,8 @@
         jnp.asarray(perm.T, BF16),
         jnp.asarray(spread, BF16),
     )
-    return grad_input.reshape(ROWS, COLS, C), gqkv, gproj, ggain[:, 0]
+    grad_input, gqkv, gproj, ggain = hand_on(*results)
+    return grad_input.reshape(ROWS, COLS, C), gqkv, gproj, ggain
 
 
 def solution(mesh):

time: 65.3 us -> 59.6 us (0.913)
  local copies, waits for them, and re-layouts: 4.9 us -> 0 us
  Pallas kernels: 59.6 us -> 58.6 us
    pallas_call x1, Pallas kernels: 59.6 us -> 55.7 us  [sublayer(): pl.pallas_call(sublayer_kernel, out_shape=(jax.ShapeDtypeStruct((TOKENS,...]
    unnamed x7 -> x0, local copies, waits for them, and re-layouts: 3.59 us -> none
    pallas_call x0 -> x1, Pallas kernels: none -> 2.93 us  [hand_on(): pl.pallas_call(hand_on_kernel, out_shape=(jax.ShapeDtypeStruct((TOKENS, C...]
    slice x1 -> x0, local copies, waits for them, and re-layouts: 1.31 us -> none  [on_device(): return (grad_input.reshape(ROWS, COLS, C), gqkv, gproj, ggain[:, 0])]
where the time goes in v4:
time: 59.6 us; the launch traced here: 59.4 us
  Pallas kernels  58.6 us (98%)
  between operations  0.82 us (1%)
    pallas_call x1, Pallas kernels, sublayer(): pl.pallas_call(sublayer_kernel, out_shape=(jax.ShapeDtypeStruct((TOKENS,...  55.7 us
    pallas_call x1, Pallas kernels, hand_on(): pl.pallas_call(hand_on_kernel, out_shape=(jax.ShapeDtypeStruct((TOKENS, C...  2.93 us

profile of v4, /device:TPU:0, one launch (start us, length us, event | category | flops | bytes accessed | tf_op | source)
XLA Modules:
  0.0 59.4 jit_solution(14468857862550541749)
XLA Ops:
  0.6 55.7 %window_grads.1 = (bf16[1152,512]{1,0:T(8,128)(2,1)}, f32[4,1536]{1,0:T(4,128)}, f32[4,512]{1,0:T(4,128)}, f32[1,128]{1,0:T(1,128)}) custom-call(bf16[1152,512]{1,0:T(8,128)(2,1)} %bitcast.4, bf16[1152,512]{1,0:T(8,128)(2,1)} %bitcast.5, f32[1,512]{1,0:T(1,128)} %bitcast.6, bf16[512,1536]{1,0:T(8,128)(2,1)} %wqkv_hbm.1, bf16[512,512]{1,0:T(8,128)(2,1)} %wproj_hbm.1, ...), custom_call_target="tpu_custom_call" | custom-call | tf_op jit(solution)/shard_map/window_grads/pallas_call | solution.py:462
  56.3 2.9 %hand_on.1 = (bf16[1152,512]{1,0:T(8,128)(2,1)}, f32[4,1536]{1,0:T(4,128)}, f32[4,512]{1,0:T(4,128)}, f32[4]{0:T(128)}) custom-call(bf16[1152,512]{1,0:T(8,128)(2,1)} %get-tuple-element.12.out_ref, f32[4,1536]{1,0:T(4,128)} %get-tuple-element.13.gqkv_ref, f32[4,512]{1,0:T(4,128)} %get-tuple-element.14.gproj_ref, f32[1,128]{1,0:T(1,128)} %get-tuple-element.15.gain_ref), custom_call_target="tpu_custom_call" | custom-call | tf_op jit(solution)/shard_map/hand_on/pallas_call | solution.py:496

commit v5 on v4

--- a/solution.py
+++ b/solution.py
@@ -22,21 +22,38 @@
 TOKENS = ROWS * COLS
 HALF_LAT = WIN_LAT // 2
 HALF_LON = WIN_LON // 2
-SIDE = 48
+SIDE = 128
+EDGE = SIDE + 32
+LAST = 208
 GROUP = 128 // HEAD
 F32 = jnp.float32
 BF16 = jnp.bfloat16
 
 
-def window_order():
-    perm = np.zeros((BAND, BAND + SIDE), np.float32)
+def orders():
+    perm = np.zeros((BAND, BAND), np.float32)
+    beside = np.zeros((BANDS, BAND - LAST, EDGE), np.float32)
+    pick = np.zeros((EDGE, TOKENS), np.float32)
     for b in range(PER_BAND):
         for r in range(WIN_LAT):
             for c in range(WIN_LON):
                 col = WIN_LON * b + HALF_LON + c
-                src = r * COLS + col if col < COLS else BAND + r * HALF_LON + col - COLS
-                perm[b * SPAN + r * WIN_LON + c, src] = 1.0
-    return perm
+                token = b * SPAN + r * WIN_LON + c
+                if col < COLS:
+                    perm[token, r * COLS + col] = 1.0
+                    continue
+                for a in range(BANDS):
+                    beside[a, token - LAST, edge_row(a * WIN_LAT + HALF_LAT + r, col - COLS)] = 1.0
+    for row in range(ROWS):
+        for c in range(HALF_LON):
+            pick[edge_row(row + (ROWS if row < HALF_LAT else 0), c), row * COLS + c] = 1.0
+    return [jnp.asarray(x, BF16) for x in (perm, perm.T, beside, beside.transpose(0, 2, 1), pick, pick.T)]
+
+
+def edge_row(row, col):
+    if row < ROWS:
+        return (row - HALF_LAT) * HALF_LON + col
+    return SIDE + (row - ROWS) * HALF_LON + col
 
 
 def nn(a, b):
@@ -51,7 +68,7 @@
     return lax.dot_general(a, b, (((0,), (0,)), ((), ())), preferred_element_type=F32)
 
 
-PARTS = ((0, 256, "zyx", "xzy"), (256, 128, "xzy", "yxz"), (384, 128, "yxz", "zyx"))
+PARTS = ((0, 256, "zyx"), (256, 256, "yxz"))
 MESH = pl.DeviceIdType.MESH
 LEAD = HALF_LAT * COLS
 
@@ -71,11 +88,11 @@
 
 
 def sublayer_kernel(
-    own_in, own_cot, gain, wqkv_hbm, wproj_hbm, perm, perm_t, spread,
+    own_in, own_cot, gain, wqkv_hbm, wproj_hbm, perm, perm_t_hbm, beside, beside_t, pick, pick_t_hbm,
     out_hbm, gqkv_ref, gproj_ref, ggain_ref,
-    ext, side, side_out, corner, corner_out, wqkv, wproj,
-    normed, inv_std, scaled, cot_win, scaled_t, att_t, qkv, grad_att, att, grad_all,
-    out_ext, back_side, top, left, back_corner, grads, mine, theirs, got0,
+    ext, side, side_out, wqkv, wproj, perm_t, pick_t,
+    normed, inv_std, scaled, cot_win, qkv, grad_att, att, grad_all,
+    out_ext, back_side, top, left, grads, mine, theirs, got0,
     out_ref, *rest,
 ):
     buffers, (local, send, recv) = rest[:-3], rest[-3:]
@@ -84,6 +101,8 @@
         pltpu.make_async_copy(own_cot, ext.at[1, pl.ds(0, TOKENS)], local.at[1]),
         pltpu.make_async_copy(wqkv_hbm, wqkv, local.at[2]),
         pltpu.make_async_copy(wproj_hbm, wproj, local.at[3]),
+        pltpu.make_async_copy(perm_t_hbm, perm_t, local.at[5]),
+        pltpu.make_async_copy(pick_t_hbm, pick_t, local.at[6]),
     ]
     for load in loads:
         load.start()
@@ -94,12 +113,13 @@
     down, up = (lat + 1) % lats, (lat + lats - 1) % lats
     east, west = (lon + 1) % lons, (lon + lons - 1) % lons
     peers = [sibling, (down, lon), (up, lon), (lat, east), (lat, west), (down, east), (up, west)]
-    for i in range(4):
-        for j in range(4):
-            for axes in ("xy", "yz", "zx") if i and j else ("x", "y", "z") if i else ():
-                if j == 0 or len(axes) == 2:
-                    steps = dict(zip(axes, (i, j)))
-                    there = {axis: (spot[axis] + steps.get(axis, 0)) % 4 for axis in "xyz"}
+    for axes in ("xy", "xz"):
+        for i in range(4):
+            for j in range(4):
+                if (i or j) and (j or axes == "xy"):
+                    there = {axis: spot[axis] for axis in "xyz"}
+                    there[axes[0]] = (spot[axes[0]] + i) % 4
+                    there[axes[1]] = (spot[axes[1]] + j) % 4
                     peers.append(device_at(there, core))
     barrier = pltpu.get_barrier_semaphore()
     for peer in peers:
@@ -120,18 +140,13 @@
     loads[0].wait()
     loads[1].wait()
     for i in range(2):
-        for a in range(BANDS):
-            rows = BAND if a < BANDS - 1 else BAND - LEAD
-            start = LEAD + a * BAND
-            side_out[i, a * SIDE : (a + 1) * SIDE] = tn(
-                spread[0:rows], ext[i, start : start + rows]
-            ).astype(BF16)
-        corner_out[i] = tn(spread[BAND - LEAD :], ext[i, 0:LEAD]).astype(BF16)
+        side_out[i] = nn(pick[...], ext[i, 0:TOKENS]).astype(BF16)
     pl.semaphore_wait(barrier, len(peers))
+    main, angle = pl.ds(0, SIDE), pl.ds(SIDE, EDGE - SIDE)
     halo = [
-        remote(side_out, side, (lat, west)),
         remote(ext.at[:, pl.ds(0, LEAD)], ext.at[:, pl.ds(TOKENS, LEAD)], (up, lon)),
-        remote(corner_out, corner, (up, west)),
+        remote(side_out.at[:, main], side.at[:, main], (lat, west)),
+        remote(side_out.at[:, angle], side.at[:, angle], (up, west)),
     ]
 
     def forward(pieces):
@@ -142,15 +157,14 @@
                 start = LEAD + a * BAND
                 src = ext[i, start : start + BAND]
                 first_row, last_row = lo // 16 * 16, -(-hi // 16) * 16
-                rows = perm[first_row:last_row]
-                if hi < BAND:
-                    got = nn(rows[:, :BAND], src)
-                else:
-                    edge = side[i, a * SIDE : (a + 1) * SIDE]
-                    if a == BANDS - 1:
-                        edge = (edge.astype(F32) + corner[i].astype(F32)).astype(BF16)
-                    got = nn(rows, jnp.concatenate([src, edge], axis=0))
-                parts.append(got[lo - first_row : hi - first_row])
+                got = nn(perm[first_row:last_row], src)[lo - first_row : hi - first_row]
+                if hi == BAND:
+                    edge = nn(beside[a], side[i])
+                    if lo < LAST:
+                        got = jnp.concatenate([got[: LAST - lo], got[LAST - lo :] + edge], axis=0)
+                    else:
+                        got = got + edge[lo - LAST :]
+                parts.append(got)
             gathered.append(jnp.concatenate(parts, axis=0))
         x, cot = gathered
         center = x - jnp.mean(x, axis=-1, keepdims=True)
@@ -231,6 +245,22 @@
         return carry
 
     lax.fori_loop(0, BANDS - 1, early, 0)
+    def weight_sums(pieces, halves, found):
+        def tokens(ref, cols):
+            parts = [ref[lo:hi, cols] for lo, hi in pieces]
+            return jnp.concatenate(parts, axis=0).astype(BF16)
+
+        if not found:
+            found += [tokens(scaled, slice(0, C)).T, tokens(att, slice(0, C)).T]
+        for half in halves:
+            lo = half * 256
+            for j in range(3):
+                yield 4 * half + j, nn(found[0], tokens(grad_all, slice(j * C + lo, j * C + lo + 256)))
+            yield 4 * half + 3, nn(found[1], tokens(cot_win, slice(lo, lo + 256)))
+
+    starts = [a * BAND for a in range(BANDS - 1)]
+    for i, value in weight_sums([(start, start + inner) for start in starts], (0, 1), []):
+        grads[i] = value
     for copy in halo:
         copy.wait_recv()
     forward([(a, inner, BAND) for a in range(BANDS - 1)])
@@ -243,23 +273,21 @@
 
     lax.fori_loop(0, PER_BAND // 2, late, 0)
 
-    scaled_t[...] = scaled[...].astype(BF16).T
-    att_t[...] = att[...].astype(BF16).T
+    late_rows = [(start + inner, start + BAND) for start in starts] + [(TOKENS - BAND, TOKENS)]
+    turned_once = []
     upper = lax.broadcasted_iota(jnp.int32, (1, 8, 1), 1) < 4
     first_core = lax.broadcasted_iota(jnp.int32, (1, 8, 1), 1) * 0 + core == 0
     first = []
     for half in range(2):
         lo = half * 256
         lanes = slice(lo, lo + 256)
-        for j in range(3):
-            cols = slice(j * C + lo, j * C + lo + 256)
-            grads[j] = nn(scaled_t[...], grad_all[:, cols].astype(BF16))
-        grads[3] = nn(att_t[...], cot_win[:, lanes].astype(BF16))
+        for i, value in weight_sums(late_rows, (half,), turned_once):
+            grads[i] += value
 
         def pack(i, carry):
             rows = pl.ds(pl.multiple_of(i * 64, 64), 64)
             chips = pl.ds(i * 8, 8)
-            t = [grads[j, rows].reshape(8, 8, 256) for j in range(4)]
+            t = [grads[4 * half + j, rows].reshape(8, 8, 256) for j in range(4)]
             turned = [pltpu.roll(x, 4, 1) for x in t]
             block = []
             for near, far in ((t, turned), (turned, t)):
@@ -274,12 +302,14 @@
             return carry
 
         lax.fori_loop(0, 8, pack, 0)
-        for start, width, _, _ in PARTS:
+        for start, width, _ in PARTS:
             if lo <= start < lo + 256:
                 span = pl.ds(start, width)
                 first.append(remote(theirs.at[:, :, span], got0.at[:, :, span], sibling))
 
-    back = []
+    back, edges = [], []
+    loads[4].wait()
+    loads[5].wait()
 
     def backward(a):
         dst = slice(a * BAND, (a + 1) * BAND)
@@ -291,25 +321,20 @@
             - norm * jnp.mean(gn * norm, axis=-1, keepdims=True)
         )
         done = (cot_win[dst] + branch).astype(BF16)
-        slab = nn(perm_t[...], done).astype(BF16)
-        out_ext[dst] = slab[:BAND]
-        edge = slice(a * SIDE, (a + 1) * SIDE)
-        back_side[edge] = slab[BAND:]
-        edge = pl.ds(a * SIDE, SIDE)
+        out_ext[dst] = nn(perm_t[...], done).astype(BF16)
+        edges.append(nn(beside_t[a], done[LAST:]))
         if a == BANDS - 1:
             back.append(remote(out_ext.at[pl.ds(TOKENS - LEAD, LEAD)], top, (down, lon)))
-            back.append(remote(back_side.at[edge], back_corner, (down, east)))
-        back.append(remote(back_side.at[edge], left.at[edge], (lat, east)))
-
-    def role(p, r, axis):
-        first_order, second_order = PARTS[p][2:]
-        return (1 - core) * int(first_order[r] == axis) + core * int(second_order[r] == axis)
+        if len(edges) == BANDS:
+            back_side[...] = (edges[0] + edges[1] + edges[2] + edges[3]).astype(BF16)
+            back.append(remote(back_side.at[main], left.at[main], (lat, east)))
+            back.append(remote(back_side.at[angle], left.at[angle], (down, east)))
 
     def by_role(p, steps):
-        return {axis: sum(role(p, r, axis) * steps[r] for r in range(3)) for axis in "xyz"}
+        return dict(zip(PARTS[p][2], steps))
 
     def my_role(p, r):
-        return sum(role(p, r, axis) * spot[axis] for axis in "xyz")
+        return spot[PARTS[p][2][r]]
 
     def peer_at(p, steps):
         moved = by_role(p, steps)
@@ -379,10 +404,9 @@
     stage0(0)
     backward(BANDS - 1)
     stage0(1)
-    stage0(2)
     for a in range(BANDS - 1):
         backward(a)
-    for p in range(3):
+    for p in range(len(PARTS)):
         stage1(p)
 
     me = lat * lons + lon
@@ -393,19 +417,14 @@
 
     for copy in back:
         copy.wait_recv()
-    for a in range(BANDS):
-        edge = nn(spread[...], left[a * SIDE : (a + 1) * SIDE])
-        rows = BAND if a < BANDS - 1 else BAND - LEAD
-        start = a * BAND
-        out_ref[LEAD + start : LEAD + start + rows] = (
-            out_ext[start : start + rows].astype(F32) + edge[:rows]
-        ).astype(BF16)
-    edge = nn(spread[...], back_corner[...])
-    out_ref[0:LEAD] = (top[...].astype(F32) + edge[BAND - LEAD :]).astype(BF16)
+    out_ref[LEAD:] = (
+        out_ext[0 : TOKENS - LEAD].astype(F32) + nn(pick_t[LEAD:, 0:SIDE], left[0:SIDE])
+    ).astype(BF16)
+    out_ref[0:LEAD] = (top[...].astype(F32) + nn(pick_t[0:LEAD], left[...])).astype(BF16)
     store = pltpu.make_async_copy(out_ref, out_hbm, local.at[4])
     store.start()
 
-    total = jnp.concatenate([stage2(p) for p in range(3)], axis=1)
+    total = jnp.concatenate([stage2(p) for p in range(len(PARTS))], axis=1)
     total = total * (1.0 / math.sqrt(TOKENS * lats * lons))
     gqkv = [total[4 * j : 4 * j + 4] for j in range(3)]
     gqkv_ref[...] = jnp.concatenate(gqkv, axis=1)
@@ -427,38 +446,35 @@
     hbm = pl.BlockSpec(memory_space=pl.ANY)
     scratch = [
         pltpu.VMEM((2, TOKENS + LEAD, C), BF16),
-        pltpu.VMEM((2, BANDS * SIDE, C), BF16),
-        pltpu.VMEM((2, BANDS * SIDE, C), BF16),
-        pltpu.VMEM((2, SIDE, C), BF16),
-        pltpu.VMEM((2, SIDE, C), BF16),
+        pltpu.VMEM((2, EDGE, C), BF16),
+        pltpu.VMEM((2, EDGE, C), BF16),
         pltpu.VMEM((C, 3 * C), BF16),
         pltpu.VMEM((C, C), BF16),
+        pltpu.VMEM((BAND, BAND), BF16),
+        pltpu.VMEM((TOKENS, EDGE), BF16),
         pltpu.VMEM((TOKENS, C), F32),
         pltpu.VMEM((TOKENS, 128), F32),
         pltpu.VMEM((TOKENS, C), F32),
         pltpu.VMEM((TOKENS, C), F32),
-        pltpu.VMEM((C, TOKENS), BF16),
-        pltpu.VMEM((C, TOKENS), BF16),
         pltpu.VMEM((TOKENS, 3 * C), F32),
         pltpu.VMEM((TOKENS, C), F32),
         pltpu.VMEM((TOKENS, C), F32),
         pltpu.VMEM((TOKENS, 3 * C), F32),
         pltpu.VMEM((TOKENS, C), BF16),
-        pltpu.VMEM((BANDS * SIDE, C), BF16),
+        pltpu.VMEM((EDGE, C), BF16),
         pltpu.VMEM((LEAD, C), BF16),
-        pltpu.VMEM((BANDS * SIDE, C), BF16),
-        pltpu.VMEM((SIDE, C), BF16),
-        pltpu.VMEM((4, C, 256), F32),
+        pltpu.VMEM((EDGE, C), BF16),
+        pltpu.VMEM((8, C, 256), F32),
         pltpu.VMEM((64, 16, C), F32),
         pltpu.VMEM((64, 16, C), BF16),
         pltpu.VMEM((64, 16, C), BF16),
         pltpu.VMEM((TOKENS, C), BF16),
     ]
-    for _, width, _, _ in PARTS:
+    for _, width, _ in PARTS:
         for dims in ((4, 4, 4), (3, 4, 4), (4, 4), (15,)):
             scratch.append(pltpu.VMEM(dims + (16, width), BF16))
         scratch.append(pltpu.VMEM((16, width), F32))
-    copies = 3 + 6 + 19 * len(PARTS)
+    copies = 3 + 3 + 19 * len(PARTS)
     return pl.pallas_call(
         sublayer_kernel,
         out_shape=(
@@ -467,11 +483,11 @@
             jax.ShapeDtypeStruct((4, C), F32),
             jax.ShapeDtypeStruct((1, 128), F32),
         ),
-        in_specs=[hbm, hbm, vmem, hbm, hbm, vmem, vmem, vmem],
+        in_specs=[hbm, hbm, vmem, hbm, hbm, vmem, hbm, vmem, vmem, vmem, hbm],
         out_specs=(hbm, vmem, vmem, vmem),
         scratch_shapes=scratch
         + [
-            pltpu.SemaphoreType.DMA((5,)),
+            pltpu.SemaphoreType.DMA((7,)),
             pltpu.SemaphoreType.DMA((copies,)),
             pltpu.SemaphoreType.DMA((copies,)),
         ],
@@ -482,47 +498,42 @@
     )(*args)
 
 
-def hand_on_kernel(out_ref, gqkv_ref, gproj_ref, gain_ref, out, gqkv, gproj, ggain, sem):
-    copy = pltpu.make_async_copy(out_ref, out, sem)
-    copy.start()
+def hand_on_kernel(out_ref, gqkv_ref, gproj_ref, gain_ref, out, gqkv, gproj, ggain):
+    out[...] = out_ref[...]
     gqkv[...] = gqkv_ref[...]
     gproj[...] = gproj_ref[...]
     ggain[...] = gain_ref[0, 0:4]
-    copy.wait()
 
 
 def hand_on(*args):
-    vmem = pl.BlockSpec(memory_space=pltpu.VMEM)
+    def whole(*shape):
+        return pl.BlockSpec(shape, lambda i: (0,) * len(shape))
+
+    tokens = pl.BlockSpec((TOKENS // 2, C), lambda i: (i, 0))
     return pl.pallas_call(
         hand_on_kernel,
+        grid=(2,),
         out_shape=(
             jax.ShapeDtypeStruct((TOKENS, C), BF16),
             jax.ShapeDtypeStruct((4, 3 * C), F32),
             jax.ShapeDtypeStruct((4, C), F32),
             jax.ShapeDtypeStruct((4,), F32),
         ),
-        in_specs=[vmem] * 4,
-        out_specs=(pl.BlockSpec(memory_space=pl.ANY), vmem, vmem, vmem),
-        scratch_shapes=[pltpu.SemaphoreType.DMA],
+        in_specs=[tokens, whole(4, 3 * C), whole(4, C), whole(1, 128)],
+        out_specs=(tokens, whole(4, 3 * C), whole(4, C), whole(4)),
+        compiler_params=pltpu.CompilerParams(vmem_limit_bytes=62 * 1024 * 1024),
         name="hand_on",
     )(*args)
 
 
 def on_device(activations, cotangent, norm_gain, qkv_weight, proj_weight):
-    perm = window_order()
-    spread = np.zeros((BAND, SIDE), np.float32)
-    for r in range(WIN_LAT):
-        for c in range(HALF_LON):
-            spread[r * COLS + c, r * HALF_LON + c] = 1.0
     results = sublayer(
         activations.reshape(TOKENS, C),
         cotangent.reshape(TOKENS, C),
         norm_gain.reshape(1, C),
         qkv_weight,
         proj_weight,
-        jnp.asarray(perm, BF16),
-        jnp.asarray(perm.T, BF16),
-        jnp.asarray(spread, BF16),
+        *orders(),
     )
     grad_input, gqkv, gproj, ggain = hand_on(*results)
     return grad_input.reshape(ROWS, COLS, C), gqkv, gproj, ggain

time: 59.6 us -> 56.8 us (0.953)
  Pallas kernels: 58.6 us -> 55.8 us
    pallas_call x1, Pallas kernels: 55.7 us -> 53.6 us  [sublayer(): pl.pallas_call(sublayer_kernel, out_shape=(jax.ShapeDtypeStruct((TOKENS,...]
    pallas_call x1, Pallas kernels: 2.93 us -> 2.16 us  [hand_on(): pl.pallas_call(hand_on_kernel, grid=(2,), out_shape=(jax.ShapeDtypeStruct...]
where the time goes in v5:
time: 56.8 us; the launch traced here: 56.5 us
  Pallas kernels  55.8 us (98%)
  between operations  0.64 us (1%)
    pallas_call x1, Pallas kernels, sublayer(): pl.pallas_call(sublayer_kernel, out_shape=(jax.ShapeDtypeStruct((TOKENS,...  53.6 us
    pallas_call x1, Pallas kernels, hand_on(): pl.pallas_call(hand_on_kernel, grid=(2,), out_shape=(jax.ShapeDtypeStruct...  2.16 us

profile of v5, /device:TPU:0, one launch (start us, length us, event | category | flops | bytes accessed | tf_op | source)
XLA Modules:
  0.0 56.5 jit_solution(14419458471655206834)
XLA Ops:
  0.6 53.6 %window_grads.1 = (bf16[1152,512]{1,0:T(8,128)(2,1)}, f32[4,1536]{1,0:T(4,128)}, f32[4,512]{1,0:T(4,128)}, f32[1,128]{1,0:T(1,128)}) custom-call(bf16[1152,512]{1,0:T(8,128)(2,1)} %bitcast.4, bf16[1152,512]{1,0:T(8,128)(2,1)} %bitcast.5, f32[1,512]{1,0:T(1,128)} %bitcast.6, bf16[512,1536]{1,0:T(8,128)(2,1)} %wqkv_hbm.1, bf16[512,512]{1,0:T(8,128)(2,1)} %wproj_hbm.1, ...), custom_call_target="tpu_custom_call" | custom-call | tf_op jit(solution)/shard_map/window_grads/pallas_call | solution.py:478
  54.3 2.2 %hand_on.1 = (bf16[1152,512]{1,0:T(8,128)(2,1)}, f32[4,1536]{1,0:T(4,128)}, f32[4,512]{1,0:T(4,128)}, f32[4]{0:T(128)}) custom-call(bf16[1152,512]{1,0:T(8,128)(2,1)} %get-tuple-element.12.out_ref, f32[4,1536]{1,0:T(4,128)} %get-tuple-element.13.gqkv_ref, f32[4,512]{1,0:T(4,128)} %get-tuple-element.14.gproj_ref, f32[1,128]{1,0:T(1,128)} %get-tuple-element.15.gain_ref), custom_call_target="tpu_custom_call" | custom-call | tf_op jit(solution)/shard_map/hand_on/pallas_call | solution.py:513

commit v6 on v5

--- a/solution.py
+++ b/solution.py
@@ -144,8 +144,8 @@
     pl.semaphore_wait(barrier, len(peers))
     main, angle = pl.ds(0, SIDE), pl.ds(SIDE, EDGE - SIDE)
     halo = [
+        remote(side_out.at[:, main], side.at[:, main], (lat, west)),
         remote(ext.at[:, pl.ds(0, LEAD)], ext.at[:, pl.ds(TOKENS, LEAD)], (up, lon)),
-        remote(side_out.at[:, main], side.at[:, main], (lat, west)),
         remote(side_out.at[:, angle], side.at[:, angle], (up, west)),
     ]
 
@@ -159,7 +159,8 @@
                 first_row, last_row = lo // 16 * 16, -(-hi // 16) * 16
                 got = nn(perm[first_row:last_row], src)[lo - first_row : hi - first_row]
                 if hi == BAND:
-                    edge = nn(beside[a], side[i])
+                    width = EDGE if a == BANDS - 1 else SIDE
+                    edge = nn(beside[a, :, 0:width], side[i, 0:width])
                     if lo < LAST:
                         got = jnp.concatenate([got[: LAST - lo], got[LAST - lo :] + edge], axis=0)
                     else:
@@ -261,11 +262,12 @@
     starts = [a * BAND for a in range(BANDS - 1)]
     for i, value in weight_sums([(start, start + inner) for start in starts], (0, 1), []):
         grads[i] = value
-    for copy in halo:
-        copy.wait_recv()
+    halo[0].wait_recv()
     forward([(a, inner, BAND) for a in range(BANDS - 1)])
+    attention([a * PER_BAND + PER_BAND - 1 for a in range(BANDS - 1)])
+    halo[1].wait_recv()
+    halo[2].wait_recv()
     forward([(BANDS - 1, 0, BAND)])
-    attention([a * PER_BAND + PER_BAND - 1 for a in range(BANDS - 1)])
 
     def late(i, carry):
         attention([(BANDS - 1) * PER_BAND + 2 * i + b for b in range(2)], edge=True)
@@ -301,7 +303,7 @@
             theirs[chips, :, lanes] = jnp.where(is_first, block[1], block[0]).astype(BF16)
             return carry
 
-        lax.fori_loop(0, 8, pack, 0)
+        lax.fori_loop(0, 8, pack, 0, unroll=2)
         for start, width, _ in PARTS:
             if lo <= start < lo + 256:
                 span = pl.ds(start, width)
@@ -356,7 +358,7 @@
             held[at] = summed0(p, chip_at(by_role(p, at))).astype(BF16)
             return carry
 
-        lax.fori_loop(0, 64, add, 0)
+        lax.fori_loop(0, 64, add, 0, unroll=4)
         for k in (2, 1, 3):
             sent[p].append(
                 remote(held.at[(my_role(p, 0) + k) % 4], got.at[k - 1], peer_at(p, (k, 0, 0)))
@@ -379,7 +381,7 @@
             nxt[i // 4, i % 4] = total(i // 4, i % 4).astype(BF16)
             return carry
 
-        lax.fori_loop(0, 16, add, 0)
+        lax.fori_loop(0, 16, add, 0, unroll=4)
         keep[...] = total(b, c)
         for i in (2, 1, 3, 0):
             for j in (2, 1, 3, 0):
@@ -401,8 +403,8 @@
             x = x + got[i].astype(F32)
         return x
 
+    backward(BANDS - 1)
     stage0(0)
-    backward(BANDS - 1)
     stage0(1)
     for a in range(BANDS - 1):
         backward(a)

time: 56.8 us -> 53.7 us (0.945)
  Pallas kernels: 55.8 us -> 52.8 us
    pallas_call x1, Pallas kernels: 53.6 us -> 50.7 us  [sublayer(): pl.pallas_call(sublayer_kernel, out_shape=(jax.ShapeDtypeStruct((TOKENS,...]
where the time goes in v6:
time: 53.7 us; the launch traced here: 53.5 us
  Pallas kernels  52.8 us (98%)
  between operations  0.64 us (1%)
    pallas_call x1, Pallas kernels, sublayer(): pl.pallas_call(sublayer_kernel, out_shape=(jax.ShapeDtypeStruct((TOKENS,...  50.7 us
    pallas_call x1, Pallas kernels, hand_on(): pl.pallas_call(hand_on_kernel, grid=(2,), out_shape=(jax.ShapeDtypeStruct...  2.16 us

profile of v6, /device:TPU:0, one launch (start us, length us, event | category | flops | bytes accessed | tf_op | source)
XLA Modules:
  0.0 53.5 jit_solution(10778849370316579059)
XLA Ops:
  0.6 50.7 %window_grads.1 = (bf16[1152,512]{1,0:T(8,128)(2,1)}, f32[4,1536]{1,0:T(4,128)}, f32[4,512]{1,0:T(4,128)}, f32[1,128]{1,0:T(1,128)}) custom-call(bf16[1152,512]{1,0:T(8,128)(2,1)} %bitcast.4, bf16[1152,512]{1,0:T(8,128)(2,1)} %bitcast.5, f32[1,512]{1,0:T(1,128)} %bitcast.6, bf16[512,1536]{1,0:T(8,128)(2,1)} %wqkv_hbm.1, bf16[512,512]{1,0:T(8,128)(2,1)} %wproj_hbm.1, ...), custom_call_target="tpu_custom_call" | custom-call | tf_op jit(solution)/shard_map/window_grads/pallas_call | solution.py:480
  51.3 2.2 %hand_on.1 = (bf16[1152,512]{1,0:T(8,128)(2,1)}, f32[4,1536]{1,0:T(4,128)}, f32[4,512]{1,0:T(4,128)}, f32[4]{0:T(128)}) custom-call(bf16[1152,512]{1,0:T(8,128)(2,1)} %get-tuple-element.12.out_ref, f32[4,1536]{1,0:T(4,128)} %get-tuple-element.13.gqkv_ref, f32[4,512]{1,0:T(4,128)} %get-tuple-element.14.gproj_ref, f32[1,128]{1,0:T(1,128)} %get-tuple-element.15.gain_ref), custom_call_target="tpu_custom_call" | custom-call | tf_op jit(solution)/shard_map/hand_on/pallas_call | solution.py:515

commit v7 on v6

--- a/solution.py
+++ b/solution.py
@@ -25,13 +25,15 @@
 SIDE = 128
 EDGE = SIDE + 32
 LAST = 208
+TWO = 2 * COLS
+PIECE = 2 * WIN_LON
 GROUP = 128 // HEAD
 F32 = jnp.float32
 BF16 = jnp.bfloat16
 
 
 def orders():
-    perm = np.zeros((BAND, BAND), np.float32)
+    perm = np.zeros((TWO, TWO), np.float32)
     beside = np.zeros((BANDS, BAND - LAST, EDGE), np.float32)
     pick = np.zeros((EDGE, TOKENS), np.float32)
     for b in range(PER_BAND):
@@ -40,7 +42,8 @@
                 col = WIN_LON * b + HALF_LON + c
                 token = b * SPAN + r * WIN_LON + c
                 if col < COLS:
-                    perm[token, r * COLS + col] = 1.0
+                    if r < 2:
+                        perm[b * PIECE + r * WIN_LON + c, r * COLS + col] = 1.0
                     continue
                 for a in range(BANDS):
                     beside[a, token - LAST, edge_row(a * WIN_LAT + HALF_LAT + r, col - COLS)] = 1.0
@@ -88,22 +91,24 @@
 
 
 def sublayer_kernel(
-    own_in, own_cot, gain, wqkv_hbm, wproj_hbm, perm, perm_t_hbm, beside, beside_t, pick, pick_t_hbm,
-    out_hbm, gqkv_ref, gproj_ref, ggain_ref,
-    ext, side, side_out, wqkv, wproj, perm_t, pick_t,
-    normed, inv_std, scaled, cot_win, qkv, grad_att, att, grad_all,
-    out_ext, back_side, top, left, grads, mine, theirs, got0,
-    out_ref, *rest,
+    own_in, own_cot, *rest,
 ):
+    fetched, rest = rest[:9], rest[9:]
+    (
+        out_hbm, gqkv_ref, gproj_ref, ggain_ref,
+        ext, side, side_out,
+        normed, inv_std, scaled, cot_win, qkv, grad_att, att, grad_all,
+        out_ext, back_side, top, left, grads, mine, theirs, got0, out_ref,
+    ) = rest[:24]
+    held_here, rest = rest[24:33], rest[33:]
+    gain, wqkv, wproj, perm, perm_t, beside, beside_t, pick, pick_t = held_here
     buffers, (local, send, recv) = rest[:-3], rest[-3:]
     loads = [
         pltpu.make_async_copy(own_in, ext.at[0, pl.ds(0, TOKENS)], local.at[0]),
         pltpu.make_async_copy(own_cot, ext.at[1, pl.ds(0, TOKENS)], local.at[1]),
-        pltpu.make_async_copy(wqkv_hbm, wqkv, local.at[2]),
-        pltpu.make_async_copy(wproj_hbm, wproj, local.at[3]),
-        pltpu.make_async_copy(perm_t_hbm, perm_t, local.at[5]),
-        pltpu.make_async_copy(pick_t_hbm, pick_t, local.at[6]),
     ]
+    for i in (7, 1, 3, 0, 2, 5, 4, 6, 8):
+        loads.append(pltpu.make_async_copy(fetched[i], held_here[i], local.at[3 + i]))
     for load in loads:
         load.start()
 
@@ -137,8 +142,8 @@
         copy.start()
         return copy
 
-    loads[0].wait()
-    loads[1].wait()
+    for load in loads[:3]:
+        load.wait()
     for i in range(2):
         side_out[i] = nn(pick[...], ext[i, 0:TOKENS]).astype(BF16)
     pl.semaphore_wait(barrier, len(peers))
@@ -155,9 +160,18 @@
             parts = []
             for a, lo, hi in pieces:
                 start = LEAD + a * BAND
-                src = ext[i, start : start + BAND]
-                first_row, last_row = lo // 16 * 16, -(-hi // 16) * 16
-                got = nn(perm[first_row:last_row], src)[lo - first_row : hi - first_row]
+                first = lo // SPAN * PIECE
+                first_row = first // 16 * 16
+                last = hi // SPAN * PIECE
+                rows = perm[first_row : -(-last // 16) * 16]
+                thirds = [
+                    nn(rows, ext[i, start + j * TWO : start + (j + 1) * TWO])[first - first_row :]
+                    for j in range(3)
+                ]
+                got = [
+                    third[at : at + PIECE] for at in range(0, last - first, PIECE) for third in thirds
+                ]
+                got = jnp.concatenate(got, axis=0)
                 if hi == BAND:
                     width = EDGE if a == BANDS - 1 else SIDE
                     edge = nn(beside[a, :, 0:width], side[i, 0:width])
@@ -236,8 +250,8 @@
             grad_all[rows, cols[1]] = grad_k[i]
             grad_all[rows, cols[2]] = grad_v[i]
 
-    loads[2].wait()
-    loads[3].wait()
+    for load in loads[3:8]:
+        load.wait()
     inner = (PER_BAND - 1) * SPAN
     forward([(a, 0, inner) for a in range(BANDS - 1)])
 
@@ -310,8 +324,8 @@
                 first.append(remote(theirs.at[:, :, span], got0.at[:, :, span], sibling))
 
     back, edges = [], []
-    loads[4].wait()
-    loads[5].wait()
+    for load in loads[8:]:
+        load.wait()
 
     def backward(a):
         dst = slice(a * BAND, (a + 1) * BAND)
@@ -322,9 +336,13 @@
             - jnp.mean(gn, axis=-1, keepdims=True)
             - norm * jnp.mean(gn * norm, axis=-1, keepdims=True)
         )
-        done = (cot_win[dst] + branch).astype(BF16)
-        out_ext[dst] = nn(perm_t[...], done).astype(BF16)
-        edges.append(nn(beside_t[a], done[LAST:]))
+        done = cot_win[dst] + branch
+        for j in range(3):
+            at = [b * SPAN + j * PIECE for b in range(PER_BAND)]
+            part = jnp.concatenate([done[i : i + PIECE] for i in at], axis=0).astype(BF16)
+            slab = slice(a * BAND + j * TWO, a * BAND + (j + 1) * TWO)
+            out_ext[slab] = nn(perm_t[...], part).astype(BF16)
+        edges.append(nn(beside_t[a], done[LAST:].astype(BF16)))
         if a == BANDS - 1:
             back.append(remote(out_ext.at[pl.ds(TOKENS - LEAD, LEAD)], top, (down, lon)))
         if len(edges) == BANDS:
@@ -423,7 +441,7 @@
         out_ext[0 : TOKENS - LEAD].astype(F32) + nn(pick_t[LEAD:, 0:SIDE], left[0:SIDE])
     ).astype(BF16)
     out_ref[0:LEAD] = (top[...].astype(F32) + nn(pick_t[0:LEAD], left[...])).astype(BF16)
-    store = pltpu.make_async_copy(out_ref, out_hbm, local.at[4])
+    store = pltpu.make_async_copy(out_ref, out_hbm, local.at[2])
     store.start()
 
     total = jnp.concatenate([stage2(p) for p in range(len(PARTS))], axis=1)
@@ -450,10 +468,6 @@
         pltpu.VMEM((2, TOKENS + LEAD, C), BF16),
         pltpu.VMEM((2, EDGE, C), BF16),
         pltpu.VMEM((2, EDGE, C), BF16),
-        pltpu.VMEM((C, 3 * C), BF16),
-        pltpu.VMEM((C, C), BF16),
-        pltpu.VMEM((BAND, BAND), BF16),
-        pltpu.VMEM((TOKENS, EDGE), BF16),
         pltpu.VMEM((TOKENS, C), F32),
         pltpu.VMEM((TOKENS, 128), F32),
         pltpu.VMEM((TOKENS, C), F32),
@@ -472,6 +486,7 @@
         pltpu.VMEM((64, 16, C), BF16),
         pltpu.VMEM((TOKENS, C), BF16),
     ]
+    scratch += [pltpu.VMEM(x.shape, x.dtype) for x in args[2:]]
     for _, width, _ in PARTS:
         for dims in ((4, 4, 4), (3, 4, 4), (4, 4), (15,)):
             scratch.append(pltpu.VMEM(dims + (16, width), BF16))
@@ -485,11 +500,11 @@
             jax.ShapeDtypeStruct((4, C), F32),
             jax.ShapeDtypeStruct((1, 128), F32),
         ),
-        in_specs=[hbm, hbm, vmem, hbm, hbm, vmem, hbm, vmem, vmem, vmem, hbm],
+        in_specs=[hbm] * 11,
         out_specs=(hbm, vmem, vmem, vmem),
         scratch_shapes=scratch
         + [
-            pltpu.SemaphoreType.DMA((7,)),
+            pltpu.SemaphoreType.DMA((12,)),
             pltpu.SemaphoreType.DMA((copies,)),
             pltpu.SemaphoreType.DMA((copies,)),
         ],

time: 53.7 us -> 52 us (0.968)
  Pallas kernels: 52.8 us -> 51.1 us
    pallas_call x1, Pallas kernels: 50.7 us -> 49 us  [sublayer(): pl.pallas_call(sublayer_kernel, out_shape=(jax.ShapeDtypeStruct((TOKENS,...]
where the time goes in v7:
time: 52 us; the launch traced here: 51.8 us
  Pallas kernels  51.1 us (98%)
  between operations  0.64 us (1%)
    pallas_call x1, Pallas kernels, sublayer(): pl.pallas_call(sublayer_kernel, out_shape=(jax.ShapeDtypeStruct((TOKENS,...  49 us
    pallas_call x1, Pallas kernels, hand_on(): pl.pallas_call(hand_on_kernel, grid=(2,), out_shape=(jax.ShapeDtypeStruct...  2.16 us

profile of v7, /device:TPU:0, one launch (start us, length us, event | category | flops | bytes accessed | tf_op | source)
XLA Modules:
  0.0 51.8 jit_solution(11462289079570073699)
XLA Ops:
  0.6 49.0 %window_grads.1 = (bf16[1152,512]{1,0:T(8,128)(2,1)}, f32[4,1536]{1,0:T(4,128)}, f32[4,512]{1,0:T(4,128)}, f32[1,128]{1,0:T(1,128)}) custom-call(bf16[1152,512]{1,0:T(8,128)(2,1)} %bitcast.4, bf16[1152,512]{1,0:T(8,128)(2,1)} %bitcast.5, f32[1,512]{1,0:T(1,128)} %bitcast.6, bf16[512,1536]{1,0:T(8,128)(2,1)} %rest_1_.1, bf16[512,512]{1,0:T(8,128)(2,1)} %rest_2_.1, ...), custom_call_target="tpu_custom_call" | custom-call | tf_op jit(solution)/shard_map/window_grads/pallas_call | solution.py:495
  49.6 2.2 %hand_on.1 = (bf16[1152,512]{1,0:T(8,128)(2,1)}, f32[4,1536]{1,0:T(4,128)}, f32[4,512]{1,0:T(4,128)}, f32[4]{0:T(128)}) custom-call(bf16[1152,512]{1,0:T(8,128)(2,1)} %get-tuple-element.12.out_ref, f32[4,1536]{1,0:T(4,128)} %get-tuple-element.13.gqkv_ref, f32[4,512]{1,0:T(4,128)} %get-tuple-element.14.gproj_ref, f32[1,128]{1,0:T(1,128)} %get-tuple-element.15.gain_ref), custom_call_target="tpu_custom_call" | custom-call | tf_op jit(solution)/shard_map/hand_on/pallas_call | solution.py:530

commit v8 on v7

--- a/solution.py
+++ b/solution.py
@@ -71,7 +71,7 @@
     return lax.dot_general(a, b, (((0,), (0,)), ((), ())), preferred_element_type=F32)
 
 
-PARTS = ((0, 256, "zyx"), (256, 256, "yxz"))
+PARTS = ((0, 256, "zyx", "yxz"), (256, 128, "yxz", "zyx"), (384, 128, "xzy", "xzy"))
 MESH = pl.DeviceIdType.MESH
 LEAD = HALF_LAT * COLS
 
@@ -118,10 +118,10 @@
     down, up = (lat + 1) % lats, (lat + lats - 1) % lats
     east, west = (lon + 1) % lons, (lon + lons - 1) % lons
     peers = [sibling, (down, lon), (up, lon), (lat, east), (lat, west), (down, east), (up, west)]
-    for axes in ("xy", "xz"):
+    for axes in ("xy", "xz", "yz"):
         for i in range(4):
             for j in range(4):
-                if (i or j) and (j or axes == "xy"):
+                if (i or j) and (j or axes == "xy") and (i or axes != "yz"):
                     there = {axis: spot[axis] for axis in "xyz"}
                     there[axes[0]] = (spot[axes[0]] + i) % 4
                     there[axes[1]] = (spot[axes[1]] + j) % 4
@@ -318,7 +318,7 @@
             return carry
 
         lax.fori_loop(0, 8, pack, 0, unroll=2)
-        for start, width, _ in PARTS:
+        for start, width, _, _ in PARTS:
             if lo <= start < lo + 256:
                 span = pl.ds(start, width)
                 first.append(remote(theirs.at[:, :, span], got0.at[:, :, span], sibling))
@@ -350,11 +350,15 @@
             back.append(remote(back_side.at[main], left.at[main], (lat, east)))
             back.append(remote(back_side.at[angle], left.at[angle], (down, east)))
 
+    def role(p, r, axis):
+        first_order, second_order = PARTS[p][2:]
+        return (1 - core) * int(first_order[r] == axis) + core * int(second_order[r] == axis)
+
     def by_role(p, steps):
-        return dict(zip(PARTS[p][2], steps))
+        return {axis: sum(role(p, r, axis) * steps[r] for r in range(3)) for axis in "xyz"}
 
     def my_role(p, r):
-        return spot[PARTS[p][2][r]]
+        return sum(role(p, r, axis) * spot[axis] for axis in "xyz")
 
     def peer_at(p, steps):
         moved = by_role(p, steps)
@@ -376,7 +380,7 @@
             held[at] = summed0(p, chip_at(by_role(p, at))).astype(BF16)
             return carry
 
-        lax.fori_loop(0, 64, add, 0, unroll=4)
+        lax.fori_loop(0, 64, add, 0, unroll=8)
         for k in (2, 1, 3):
             sent[p].append(
                 remote(held.at[(my_role(p, 0) + k) % 4], got.at[k - 1], peer_at(p, (k, 0, 0)))
@@ -399,7 +403,7 @@
             nxt[i // 4, i % 4] = total(i // 4, i % 4).astype(BF16)
             return carry
 
-        lax.fori_loop(0, 16, add, 0, unroll=4)
+        lax.fori_loop(0, 16, add, 0, unroll=8)
         keep[...] = total(b, c)
         for i in (2, 1, 3, 0):
             for j in (2, 1, 3, 0):
@@ -424,6 +428,7 @@
     backward(BANDS - 1)
     stage0(0)
     stage0(1)
+    stage0(2)
     for a in range(BANDS - 1):
         backward(a)
     for p in range(len(PARTS)):
@@ -444,6 +449,8 @@
     store = pltpu.make_async_copy(out_ref, out_hbm, local.at[2])
     store.start()
 
+    for copy in halo + first + back + [c for part in sent for c in part[:3]]:
+        copy.wait_send()
     total = jnp.concatenate([stage2(p) for p in range(len(PARTS))], axis=1)
     total = total * (1.0 / math.sqrt(TOKENS * lats * lons))
     gqkv = [total[4 * j : 4 * j + 4] for j in range(3)]
@@ -456,7 +463,7 @@
     diagonal = lax.broadcasted_iota(jnp.int32, (4, 128), 0)
     diagonal = diagonal == lax.broadcasted_iota(jnp.int32, (4, 128), 1)
     ggain_ref[...] = jnp.sum(jnp.where(diagonal, dots, 0.0), axis=0, keepdims=True)
-    for copy in halo + first + back + [c for part in sent for c in part]:
+    for copy in [c for part in sent for c in part[3:]]:
         copy.wait_send()
     store.wait()
 
@@ -487,7 +494,7 @@
         pltpu.VMEM((TOKENS, C), BF16),
     ]
     scratch += [pltpu.VMEM(x.shape, x.dtype) for x in args[2:]]
-    for _, width, _ in PARTS:
+    for _, width, _, _ in PARTS:
         for dims in ((4, 4, 4), (3, 4, 4), (4, 4), (15,)):
             scratch.append(pltpu.VMEM(dims + (16, width), BF16))
         scratch.append(pltpu.VMEM((16, width), F32))

time: 52 us -> 50.3 us (0.967)
  Pallas kernels: 51.1 us -> 49.6 us
    pallas_call x1, Pallas kernels: 49 us -> 47.4 us  [sublayer(): pl.pallas_call(sublayer_kernel, out_shape=(jax.ShapeDtypeStruct((TOKENS,...]
where the time goes in v8:
time: 50.3 us; the launch traced here: 50.2 us
  Pallas kernels  49.6 us (99%)
  between operations  0.64 us (1%)
    pallas_call x1, Pallas kernels, sublayer(): pl.pallas_call(sublayer_kernel, out_shape=(jax.ShapeDtypeStruct((TOKENS,...  47.4 us
    pallas_call x1, Pallas kernels, hand_on(): pl.pallas_call(hand_on_kernel, grid=(2,), out_shape=(jax.ShapeDtypeStruct...  2.16 us

profile of v8, /device:TPU:0, one launch (start us, length us, event | category | flops | bytes accessed | tf_op | source)
XLA Modules:
  0.0 50.2 jit_solution(12330381744778524886)
XLA Ops:
  0.6 47.4 %window_grads.1 = (bf16[1152,512]{1,0:T(8,128)(2,1)}, f32[4,1536]{1,0:T(4,128)}, f32[4,512]{1,0:T(4,128)}, f32[1,128]{1,0:T(1,128)}) custom-call(bf16[1152,512]{1,0:T(8,128)(2,1)} %bitcast.4, bf16[1152,512]{1,0:T(8,128)(2,1)} %bitcast.5, f32[1,512]{1,0:T(1,128)} %bitcast.6, bf16[512,1536]{1,0:T(8,128)(2,1)} %rest_1_.1, bf16[512,512]{1,0:T(8,128)(2,1)} %rest_2_.1, ...), custom_call_target="tpu_custom_call" | custom-call | tf_op jit(solution)/shard_map/window_grads/pallas_call | solution.py:502
  48.0 2.2 %hand_on.1 = (bf16[1152,512]{1,0:T(8,128)(2,1)}, f32[4,1536]{1,0:T(4,128)}, f32[4,512]{1,0:T(4,128)}, f32[4]{0:T(128)}) custom-call(bf16[1152,512]{1,0:T(8,128)(2,1)} %get-tuple-element.12.out_ref, f32[4,1536]{1,0:T(4,128)} %get-tuple-element.13.gqkv_ref, f32[4,512]{1,0:T(4,128)} %get-tuple-element.14.gproj_ref, f32[1,128]{1,0:T(1,128)} %get-tuple-element.15.gain_ref), custom_call_target="tpu_custom_call" | custom-call | tf_op jit(solution)/shard_map/hand_on/pallas_call | solution.py:537

commit v9 on v8

--- a/solution.py
+++ b/solution.py
@@ -323,32 +323,33 @@
                 span = pl.ds(start, width)
                 first.append(remote(theirs.at[:, :, span], got0.at[:, :, span], sibling))
 
-    back, edges = [], []
+    back = []
     for load in loads[8:]:
         load.wait()
 
-    def backward(a):
-        dst = slice(a * BAND, (a + 1) * BAND)
-        gn = nt(grad_all[dst].astype(BF16), wqkv[...]) * gain[...]
-        norm = normed[dst]
-        branch = inv_std[dst][:, 0:1] * (
+    def norm_grads(pieces):
+        def tokens(ref):
+            return jnp.concatenate([ref[lo:hi] for lo, hi in pieces], axis=0)
+
+        gn = nt(tokens(grad_all).astype(BF16), wqkv[...]) * gain[...]
+        norm = tokens(normed)
+        branch = tokens(inv_std)[:, 0:1] * (
             gn
             - jnp.mean(gn, axis=-1, keepdims=True)
             - norm * jnp.mean(gn * norm, axis=-1, keepdims=True)
         )
-        done = cot_win[dst] + branch
+        done = tokens(cot_win) + branch
+        at = 0
+        for lo, hi in pieces:
+            normed[lo:hi] = done[at : at + hi - lo]
+            at += hi - lo
+
+    def to_slab(a):
         for j in range(3):
-            at = [b * SPAN + j * PIECE for b in range(PER_BAND)]
-            part = jnp.concatenate([done[i : i + PIECE] for i in at], axis=0).astype(BF16)
+            at = [a * BAND + b * SPAN + j * PIECE for b in range(PER_BAND)]
+            part = jnp.concatenate([normed[i : i + PIECE] for i in at], axis=0).astype(BF16)
             slab = slice(a * BAND + j * TWO, a * BAND + (j + 1) * TWO)
             out_ext[slab] = nn(perm_t[...], part).astype(BF16)
-        edges.append(nn(beside_t[a], done[LAST:].astype(BF16)))
-        if a == BANDS - 1:
-            back.append(remote(out_ext.at[pl.ds(TOKENS - LEAD, LEAD)], top, (down, lon)))
-        if len(edges) == BANDS:
-            back_side[...] = (edges[0] + edges[1] + edges[2] + edges[3]).astype(BF16)
-            back.append(remote(back_side.at[main], left.at[main], (lat, east)))
-            back.append(remote(back_side.at[angle], left.at[angle], (down, east)))
 
     def role(p, r, axis):
         first_order, second_order = PARTS[p][2:]
@@ -425,12 +426,23 @@
             x = x + got[i].astype(F32)
         return x
 
-    backward(BANDS - 1)
+    norm_grads([(TOKENS - BAND, TOKENS)])
+    to_slab(BANDS - 1)
+    back.append(remote(out_ext.at[pl.ds(TOKENS - LEAD, LEAD)], top, (down, lon)))
     stage0(0)
     stage0(1)
     stage0(2)
+    norm_grads([(start + inner, start + BAND) for start in starts])
+    edges = jnp.zeros((EDGE, C), F32)
+    for a in range(BANDS):
+        rows = normed[a * BAND + LAST : (a + 1) * BAND].astype(BF16)
+        edges = edges + nn(beside_t[a], rows)
+    back_side[...] = edges.astype(BF16)
+    back.append(remote(back_side.at[main], left.at[main], (lat, east)))
+    back.append(remote(back_side.at[angle], left.at[angle], (down, east)))
+    norm_grads([(start, start + inner) for start in starts])
     for a in range(BANDS - 1):
-        backward(a)
+        to_slab(a)
     for p in range(len(PARTS)):
         stage1(p)
 

time: 50.3 us -> 50.4 us (level)
  no operation moved by 1% of the time
where the time goes in v9:
time: 50.4 us; the launch traced here: 50.2 us
  Pallas kernels  49.6 us (98%)
  between operations  0.64 us (1%)
    pallas_call x1, Pallas kernels, sublayer(): pl.pallas_call(sublayer_kernel, out_shape=(jax.ShapeDtypeStruct((TOKENS,...  47.4 us
    pallas_call x1, Pallas kernels, hand_on(): pl.pallas_call(hand_on_kernel, grid=(2,), out_shape=(jax.ShapeDtypeStruct...  2.16 us

profile of v9, /device:TPU:0, one launch (start us, length us, event | category | flops | bytes accessed | tf_op | source)
XLA Modules:
  0.0 50.2 jit_solution(15639219502550038856)
XLA Ops:
  0.6 47.4 %window_grads.1 = (bf16[1152,512]{1,0:T(8,128)(2,1)}, f32[4,1536]{1,0:T(4,128)}, f32[4,512]{1,0:T(4,128)}, f32[1,128]{1,0:T(1,128)}) custom-call(bf16[1152,512]{1,0:T(8,128)(2,1)} %bitcast.4, bf16[1152,512]{1,0:T(8,128)(2,1)} %bitcast.5, f32[1,512]{1,0:T(1,128)} %bitcast.6, bf16[512,1536]{1,0:T(8,128)(2,1)} %rest_1_.1, bf16[512,512]{1,0:T(8,128)(2,1)} %rest_2_.1, ...), custom_call_target="tpu_custom_call" | custom-call | tf_op jit(solution)/shard_map/window_grads/pallas_call | solution.py:514
  48.1 2.2 %hand_on.1 = (bf16[1152,512]{1,0:T(8,128)(2,1)}, f32[4,1536]{1,0:T(4,128)}, f32[4,512]{1,0:T(4,128)}, f32[4]{0:T(128)}) custom-call(bf16[1152,512]{1,0:T(8,128)(2,1)} %get-tuple-element.12.out_ref, f32[4,1536]{1,0:T(4,128)} %get-tuple-element.13.gqkv_ref, f32[4,512]{1,0:T(4,128)} %get-tuple-element.14.gproj_ref, f32[1,128]{1,0:T(1,128)} %get-tuple-element.15.gain_ref), custom_call_target="tpu_custom_call" | custom-call | tf_op jit(solution)/shard_map/hand_on/pallas_call | solution.py:549

commit v10 on v9

--- a/solution.py
+++ b/solution.py
@@ -452,14 +452,22 @@
     w_rows = nn(picked.astype(BF16), wqkv[...])
     gain_rows = jnp.sum(picked * gain[...], axis=1, keepdims=True)
 
-    for copy in back:
-        copy.wait_recv()
-    out_ref[LEAD:] = (
-        out_ext[0 : TOKENS - LEAD].astype(F32) + nn(pick_t[LEAD:, 0:SIDE], left[0:SIDE])
-    ).astype(BF16)
-    out_ref[0:LEAD] = (top[...].astype(F32) + nn(pick_t[0:LEAD], left[...])).astype(BF16)
-    store = pltpu.make_async_copy(out_ref, out_hbm, local.at[2])
-    store.start()
+    stores = []
+
+    def put(lo, hi, value):
+        out_ref[lo:hi] = value.astype(BF16)
+        rows = pl.ds(lo, hi - lo)
+        copy = pltpu.make_async_copy(out_ref.at[rows], out_hbm.at[rows], local.at[12 + len(stores)])
+        copy.start()
+        stores.append(copy)
+
+    back[1].wait_recv()
+    for lo in range(LEAD, TOKENS, 336):
+        hi = lo + 336
+        put(lo, hi, out_ext[lo - LEAD : hi - LEAD].astype(F32) + nn(pick_t[lo:hi, 0:SIDE], left[0:SIDE]))
+    back[0].wait_recv()
+    back[2].wait_recv()
+    put(0, LEAD, top[...].astype(F32) + nn(pick_t[0:LEAD], left[...]))
 
     for copy in halo + first + back + [c for part in sent for c in part[:3]]:
         copy.wait_send()
@@ -477,7 +485,8 @@
     ggain_ref[...] = jnp.sum(jnp.where(diagonal, dots, 0.0), axis=0, keepdims=True)
     for copy in [c for part in sent for c in part[3:]]:
         copy.wait_send()
-    store.wait()
+    for copy in stores:
+        copy.wait()
 
 
 def sublayer(*args):
@@ -523,7 +532,7 @@
         out_specs=(hbm, vmem, vmem, vmem),
         scratch_shapes=scratch
         + [
-            pltpu.SemaphoreType.DMA((12,)),
+            pltpu.SemaphoreType.DMA((16,)),
             pltpu.SemaphoreType.DMA((copies,)),
             pltpu.SemaphoreType.DMA((copies,)),
         ],

time: 50.4 us -> 50.4 us (level)
  no operation moved by 1% of the time
where the time goes in v10:
time: 50.4 us; the launch traced here: 50.3 us
  Pallas kernels  49.6 us (98%)
  between operations  0.64 us (1%)
    pallas_call x1, Pallas kernels, sublayer(): pl.pallas_call(sublayer_kernel, out_shape=(jax.ShapeDtypeStruct((TOKENS,...  47.5 us
    pallas_call x1, Pallas kernels, hand_on(): pl.pallas_call(hand_on_kernel, grid=(2,), out_shape=(jax.ShapeDtypeStruct...  2.16 us

profile of v10, /device:TPU:0, one launch (start us, length us, event | category | flops | bytes accessed | tf_op | source)
XLA Modules:
  0.0 50.3 jit_solution(3453006014459705613)
XLA Ops:
  0.6 47.5 %window_grads.1 = (bf16[1152,512]{1,0:T(8,128)(2,1)}, f32[4,1536]{1,0:T(4,128)}, f32[4,512]{1,0:T(4,128)}, f32[1,128]{1,0:T(1,128)}) custom-call(bf16[1152,512]{1,0:T(8,128)(2,1)} %bitcast.4, bf16[1152,512]{1,0:T(8,128)(2,1)} %bitcast.5, f32[1,512]{1,0:T(1,128)} %bitcast.6, bf16[512,1536]{1,0:T(8,128)(2,1)} %rest_1_.1, bf16[512,512]{1,0:T(8,128)(2,1)} %rest_2_.1, ...), custom_call_target="tpu_custom_call" | custom-call | tf_op jit(solution)/shard_map/window_grads/pallas_call | solution.py:523
  48.1 2.2 %hand_on.1 = (bf16[1152,512]{1,0:T(8,128)(2,1)}, f32[4,1536]{1,0:T(4,128)}, f32[4,512]{1,0:T(4,128)}, f32[4]{0:T(128)}) custom-call(bf16[1152,512]{1,0:T(8,128)(2,1)} %get-tuple-element.12.out_ref, f32[4,1536]{1,0:T(4,128)} %get-tuple-element.13.gqkv_ref, f32[4,512]{1,0:T(4,128)} %get-tuple-element.14.gproj_ref, f32[1,128]{1,0:T(1,128)} %get-tuple-element.15.gain_ref), custom_call_target="tpu_custom_call" | custom-call | tf_op jit(solution)/shard_map/hand_on/pallas_call | solution.py:558
